TPU v7x, 256 devices: a whole 4x4x8 slice. The times are simulated.
256 devices in a mesh: ctx: 64 (over y, z, core), head: 4 (over x).
Axes of the slice: x: 4, y: 4, z: 8, core: 2. Of those that a mesh axis runs over, the one named last changes fastest.
Arguments:
- query_in: bfloat16 [8192, 4096], P('ctx', 'head'), may hold values from -6 to 6
- key_in: bfloat16 [8192, 4096], P('ctx', 'head'), may hold values from -6 to 6
- value_in: bfloat16 [8192, 4096], P('ctx', 'head')
- out_grad: bfloat16 [8192, 4096], P('ctx', 'head'), may hold values from -6 to 6
- chain_order: int32 [8192], P('ctx'), may hold values from 0 to 8191, as said below
- load_order: int32 [8192], P('ctx'), may hold values from 0 to 8191, as said below
- doc_lengths: int32 [128], replicated, may hold values from 1 to 2048, 8192 in all
Outputs:
- attended: bfloat16 [8192, 4096], P('ctx', 'head')
- query_grad: bfloat16 [8192, 4096], P('ctx', 'head')
- key_grad: bfloat16 [8192, 4096], P('ctx', 'head')
- value_grad: bfloat16 [8192, 4096], P('ctx', 'head')
Inputs may be any that keep to these rules, and one draw needn't show every extreme that they name: `chain_order`: A permutation of the chain positions; load_order is its inverse. The number of tokens that ctx shard s loads and that belong to ctx shard d (chain positions d * 128 to d * 128 + 127) depends only on d - s modulo the number of shards; it is 1 to 4, and exactly 4 for one difference. `load_order`: the inverse of chain_order.
All inputs are finite; a program needn't handle non-finite values.
Results may differ from a plain program's by a relative error of at most 0.0059.
Values may be sent and summed in bfloat16 or wider, within the bound.
A program may use at most 192 MiB of HBM per device.

v0:
```python
import jax
import jax.numpy as jnp
from jax import lax
from jax.sharding import PartitionSpec as P

HEAD_DIM = 128
FEATURES = 4096


epsilon = 1e-06


def carried_in(value, axis, join, neutral, backward):
    count, mine = (lax.axis_size(axis), lax.axis_index(axis))
    pieces = jax.tree.map(lambda part: lax.all_gather(part, axis), value)
    if backward:
        pieces = jax.tree.map(lambda part: part[::-1], pieces)
        mine = count - 1 - mine
    subtotal = jax.tree.map(
        lambda part, zero: jnp.full_like(part, 0) + jnp.asarray(zero, part.dtype), value, neutral
    )

    def step(position, subtotal):
        longer = join(subtotal, jax.tree.map(lambda part: part[position], pieces))
        return jax.tree.map(lambda new, old: jnp.where(position < mine, new, old), longer, subtotal)

    return lax.fori_loop(0, count - 1, step, subtotal)


def rank_within(groups, values):
    same_group = groups[:, None] == groups[None, :]
    before = values[None, :] < values[:, None]
    return jnp.sum((same_group & before).astype(jnp.int32), axis=1)


def pack_rows(rows_in, slot_index, slot_total):
    return jnp.zeros((slot_total, rows_in.shape[1]), rows_in.dtype).at[slot_index].set(rows_in)


def doc_index(positions, doc_ends):
    return jnp.sum((doc_ends[None, :] <= positions[:, None]).astype(jnp.int32), axis=1)


def chain_combine(earlier, later_one):
    return (later_one[0] + (1.0 - later_one[1]) * earlier[0], jnp.maximum(earlier[1], later_one[1]))


def body(query_in, key_in, value_in, out_grad, chain_order, load_order, doc_lengths):
    row_count, width_dev = query_in.shape
    heads_dev = width_dev // HEAD_DIM
    shards = lax.axis_size("ctx")
    capacity = 2 * row_count // shards
    slot_total = shards * capacity
    local_index = jnp.arange(row_count, dtype=jnp.int32)
    dest_dev = chain_order // row_count
    send_slot = dest_dev * capacity + rank_within(dest_dev, local_index)
    source_dev = load_order // row_count
    recv_slot = source_dev * capacity + rank_within(source_dev, load_order)

    def arrive(packed):
        return packed[recv_slot]

    def depart(packed):
        return packed[send_slot]

    arrived = (
        lax.all_to_all(
            pack_rows(query_in, send_slot, slot_total),
            "ctx",
            split_axis=0,
            concat_axis=0,
            tiled=True,
        ),
        lax.all_to_all(
            pack_rows(key_in, send_slot, slot_total), "ctx", split_axis=0, concat_axis=0, tiled=True
        ),
        lax.all_to_all(
            pack_rows(value_in, send_slot, slot_total),
            "ctx",
            split_axis=0,
            concat_axis=0,
            tiled=True,
        ),
        lax.all_to_all(
            pack_rows(out_grad, send_slot, slot_total),
            "ctx",
            split_axis=0,
            concat_axis=0,
            tiled=True,
        ),
    )
    query_rows, key_rows, value_rows, grad_rows = jax.tree.map(arrive, arrived)
    query_heads = query_rows.reshape(row_count, heads_dev, HEAD_DIM)
    key_heads = key_rows.reshape(row_count, heads_dev, HEAD_DIM)
    value_heads = value_rows.reshape(row_count, heads_dev, HEAD_DIM)
    doc_ends = jnp.cumsum(doc_lengths)
    first_row = lax.axis_index("ctx") * row_count
    docs_here = doc_index(first_row + local_index, doc_ends)
    border = doc_index(first_row + jnp.array([-1, row_count], jnp.int32), doc_ends)
    carry_in = (docs_here == border[0]).astype(jnp.float32)
    onward = docs_here == border[1]
    onward_wide = onward.astype(jnp.float32)
    has_start = (docs_here[-1] != border[0]).astype(jnp.float32)
    causal = local_index[None, :] <= local_index[:, None]
    within = (causal & (docs_here[:, None] == docs_here[None, :])).astype(jnp.float32)
    kept_values = jnp.where(onward[:, None, None], value_heads, jnp.zeros_like(value_heads))
    forward_part = jnp.einsum(
        "tha,thb->hab", key_heads, kept_values, preferred_element_type=jnp.float32
    )
    identity = (jnp.zeros_like(forward_part), jnp.zeros((), jnp.float32))
    state_in, unused_flag = carried_in(
        (forward_part, has_start), "ctx", chain_combine, identity, False
    )
    scores = jnp.einsum("sha,tha->hst", query_heads, key_heads, preferred_element_type=jnp.float32)
    attn_low = (scores * within[None]).astype(jnp.bfloat16)
    state_low = state_in.astype(jnp.bfloat16)
    carried = jnp.einsum("sha,hab->shb", query_heads, state_low, preferred_element_type=jnp.float32)
    raw_out = (
        jnp.einsum("hst,thb->shb", attn_low, value_heads, preferred_element_type=jnp.float32)
        + carry_in[:, None, None] * carried
    )
    squares = jnp.sum(raw_out * raw_out, axis=(1, 2))
    grad_wide = grad_rows.reshape(row_count, heads_dev, HEAD_DIM).astype(jnp.float32)
    total_sq = lax.psum(squares, "head")
    root_mean = jnp.sqrt(total_sq / FEATURES + epsilon)
    normed = raw_out / root_mean[:, None, None]
    inner_mean = lax.psum(jnp.sum(grad_wide * normed, axis=(1, 2)), "head") / FEATURES
    attended_rows = normed.astype(jnp.bfloat16).reshape(row_count, width_dev)
    dgrad = ((grad_wide - normed * inner_mean[:, None, None]) / root_mean[:, None, None]).astype(
        jnp.bfloat16
    )
    kept_grad = jnp.where(carry_in[:, None, None] > 0, dgrad, jnp.zeros_like(dgrad))
    reverse_part = jnp.einsum(
        "tha,thb->hab", query_heads, kept_grad, preferred_element_type=jnp.float32
    )
    reverse_in, unused_back = carried_in(
        (reverse_part, has_start), "ctx", chain_combine, identity, True
    )
    mixed = jnp.einsum("shb,thb->hst", dgrad, value_heads, preferred_element_type=jnp.float32)
    mixed_low = (mixed * within[None]).astype(jnp.bfloat16)
    query_out = jnp.einsum(
        "hst,tha->sha", mixed_low, key_heads, preferred_element_type=jnp.float32
    ) + carry_in[:, None, None] * jnp.einsum(
        "shb,hab->sha", dgrad, state_low, preferred_element_type=jnp.float32
    )
    reverse_low = reverse_in.astype(jnp.bfloat16)
    key_out = jnp.einsum(
        "hst,sha->tha", mixed_low, query_heads, preferred_element_type=jnp.float32
    ) + onward_wide[:, None, None] * jnp.einsum(
        "thb,hab->tha", value_heads, reverse_low, preferred_element_type=jnp.float32
    )
    value_out = jnp.einsum(
        "hst,shb->thb", attn_low, dgrad, preferred_element_type=jnp.float32
    ) + onward_wide[:, None, None] * jnp.einsum(
        "tha,hab->thb", key_heads, reverse_low, preferred_element_type=jnp.float32
    )
    query_low = query_out.astype(jnp.bfloat16).reshape(row_count, width_dev)
    key_low = key_out.astype(jnp.bfloat16).reshape(row_count, width_dev)
    value_low = value_out.astype(jnp.bfloat16).reshape(row_count, width_dev)
    returned = (
        lax.all_to_all(
            pack_rows(attended_rows, recv_slot, slot_total),
            "ctx",
            split_axis=0,
            concat_axis=0,
            tiled=True,
        ),
        lax.all_to_all(
            pack_rows(query_low, recv_slot, slot_total),
            "ctx",
            split_axis=0,
            concat_axis=0,
            tiled=True,
        ),
        lax.all_to_all(
            pack_rows(key_low, recv_slot, slot_total),
            "ctx",
            split_axis=0,
            concat_axis=0,
            tiled=True,
        ),
        lax.all_to_all(
            pack_rows(value_low, recv_slot, slot_total),
            "ctx",
            split_axis=0,
            concat_axis=0,
            tiled=True,
        ),
    )
    attended, query_grad, key_grad, value_grad = jax.tree.map(depart, returned)
    return (attended, query_grad, key_grad, value_grad)


def solution(mesh):
    return jax.shard_map(
        body,
        mesh=mesh,
        in_specs=(
            P("ctx", "head"),
            P("ctx", "head"),
            P("ctx", "head"),
            P("ctx", "head"),
            P("ctx"),
            P("ctx"),
            P(),
        ),
        out_specs=(P("ctx", "head"), P("ctx", "head"), P("ctx", "head"), P("ctx", "head")),
        check_vma=False,
    )
```

profile of v0, /device:TPU:1, one launch (start us, length us, event | category | flops | bytes accessed | tf_op | source)
XLA Modules:
  0.0 849.9 jit_solution(10434222849330634582)
XLA Ops:
  8.7 1.7 scatter_custom_fusion.2
  11.4 13.2 %all-to-all-start.2 = ((bf16[64,4,1024]{2,1,0:T(4,128)(2,1)}), bf16[64,4,1024]{2,1,0:T(4,128)(2,1)S(1)}, u32[]{:S(2)}, u32[]{:S(2)}) async-start(bf16[64,4,1024]{2,1,0:T(4,128)(2,1)} %all_to_all.70), calls=%async_computation.2 | async-start | bytes 1048576 | tf_op jit(solution)/shard_map/all_to_all | solution.py:74
  24.6 1.7 scatter_custom_fusion
  28.9 13.0 %all-to-all-done.2 = bf16[64,4,1024]{2,1,0:T(4,128)(2,1)S(1)} async-done(((bf16[64,4,1024]{2,1,0:T(4,128)(2,1)}), bf16[64,4,1024]{2,1,0:T(4,128)(2,1)S(1)}, u32[]{:S(2)}, u32[]{:S(2)}) %all-to-all-start.2) | async-done | bytes 524320 | tf_op jit(solution)/shard_map/all_to_all | solution.py:74
  41.9 6.3 all-to-all-start
  54.2 11.3 %all-to-all-done = bf16[64,4,1024]{2,1,0:T(4,128)(2,1)S(1)} async-done(((bf16[64,4,1024]{2,1,0:T(4,128)(2,1)}), bf16[64,4,1024]{2,1,0:T(4,128)(2,1)S(1)}, u32[]{:S(2)}, u32[]{:S(2)}) %all-to-all-start) | async-done | bytes 524320 | tf_op jit(solution)/shard_map/all_to_all | solution.py:77
  67.8 1.7 scatter_custom_fusion.1
  70.5 6.3 all-to-all-start.1
  76.8 1.7 scatter_custom_fusion.4
  79.6 19.3 %all-to-all-done.1 = bf16[64,4,1024]{2,1,0:T(4,128)(2,1)S(1)} async-done(((bf16[64,4,1024]{2,1,0:T(4,128)(2,1)}), bf16[64,4,1024]{2,1,0:T(4,128)(2,1)S(1)}, u32[]{:S(2)}, u32[]{:S(2)}) %all-to-all-start.1) | async-done | bytes 524320 | tf_op jit(solution)/shard_map/all_to_all | solution.py:67
  98.9 6.2 all-to-all-start.4
  109.1 134.4 %all-reduce = f32[64]{0:T(128)S(1)} all-reduce(f32[64]{0:T(128)S(1)} %dynamic-update-slice), channel_id=1, replica_groups=mesh['ctx'=64,'head'=4] {'ctx'}, use_global_device_ids=true, to_apply=%add | all-reduce | flops 64 | bytes 512
  247.3 172.8 %while.28 = (s32[]{:T(128)}, f32[8,128,128]{2,1,0:T(8,128)S(1)}, s32[]{:T(128)}, f32[64,8,128,128]{3,2,1,0:T(8,128)}, f32[64]{0:T(128)S(1)}, /*index=5*/s32[]{:T(128)}, f32[1]{0:T(128)}, s32[]{:T(128)}) while((s32[]{:T(128)}, f32[8,128,128]{2,1,0:T(8,128)S(1)}, s32[]{:T(128)}, f32[64,8,128,128]{3,2,1,0:T(8,128)}, ...), condition=%wide.region_9.10_spmd.clone, body=%wide.region_8.9_spmd.clone.sunk | while | flops 524293 | bytes 1573009 | solution.py:27
  421.5 8.4 psum.14
  430.1 6.0 psum.15
  440.6 8.8 %all-to-all-start.5 = ((bf16[64,4,1024]{2,1,0:T(4,128)(2,1)}), bf16[64,4,1024]{2,1,0:T(4,128)(2,1)}, u32[]{:S(2)}, u32[]{:S(2)}) async-start(bf16[64,4,1024]{2,1,0:T(4,128)(2,1)} %all_to_all.79), calls=%async_computation.5 | async-start | bytes 1048576 | tf_op jit(solution)/shard_map/all_to_all | solution.py:168
  452.2 133.2 %all-gather.7.cloned.1.call-done = f32[512,128,128]{2,1,0:T(8,128)} async-done(((f32[8,128,128]{2,1,0:T(8,128)}), f32[512,128,128]{2,1,0:T(8,128)}) %all-gather.7.cloned.1.call-update) | async-done | bytes 33554448 | tf_op jit(solution)/shard_map/all_gather | solution.py:15
  585.5 23.0 %rev.6 = f32[64,8,128,128]{3,2,1,0:T(8,128)} reverse(f32[64,8,128,128]{3,2,1,0:T(8,128)} %bitcast.91), dimensions={0} | reverse | bytes 67108864 | tf_op jit(solution)/shard_map/rev | solution.py:17
  608.4 5.9 all-to-all-start.3
  614.4 173.1 %while.29 = (s32[]{:T(128)}, f32[8,128,128]{2,1,0:T(8,128)S(1)}, s32[]{:T(128)}, f32[64,8,128,128]{3,2,1,0:T(8,128)}, f32[64]{0:T(128)S(1)}, /*index=5*/s32[]{:T(128)}, f32[1]{0:T(128)}, s32[]{:T(128)}) while((s32[]{:T(128)}, f32[8,128,128]{2,1,0:T(8,128)S(1)}, s32[]{:T(128)}, f32[64,8,128,128]{3,2,1,0:T(8,128)}, ...), condition=%wide.region_18.19_spmd.clone, body=%wide.region_17.18_spmd.clone.sunk | while | flops 524293 | bytes 1573009 | solution.py:27
  618.4 1.5 fusion.80
  621.1 1.5 fusion.80
  626.6 1.5 fusion.80
  632.1 1.5 fusion.80
  790.1 10.3 %all-to-all-start.6 = ((bf16[64,4,1024]{2,1,0:T(4,128)(2,1)}), bf16[64,4,1024]{2,1,0:T(4,128)(2,1)S(1)}, u32[]{:S(2)}, u32[]{:S(2)}) async-start(bf16[64,4,1024]{2,1,0:T(4,128)(2,1)} %all_to_all.82), calls=%async_computation.6 | async-start | bytes 1048576 | tf_op jit(solution)/shard_map/all_to_all | solution.py:175
  803.5 14.3 %all-to-all-done.6 = bf16[64,4,1024]{2,1,0:T(4,128)(2,1)S(1)} async-done(((bf16[64,4,1024]{2,1,0:T(4,128)(2,1)}), bf16[64,4,1024]{2,1,0:T(4,128)(2,1)S(1)}, u32[]{:S(2)}, u32[]{:S(2)}) %all-to-all-start.6) | async-done | bytes 524320 | tf_op jit(solution)/shard_map/all_to_all | solution.py:175
  817.8 6.3 all-to-all-start.7
  825.3 1.6 gather_fusion.5
  827.0 1.6 gather_fusion.3
  828.6 1.6 gather_fusion.6
  830.2 11.2 %all-to-all-done.7 = bf16[64,4,1024]{2,1,0:T(4,128)(2,1)S(1)} async-done(((bf16[64,4,1024]{2,1,0:T(4,128)(2,1)}), bf16[64,4,1024]{2,1,0:T(4,128)(2,1)S(1)}, u32[]{:S(2)}, u32[]{:S(2)}) %all-to-all-start.7) | async-done | bytes 524320 | tf_op jit(solution)/shard_map/all_to_all | solution.py:182
  841.5 1.6 gather_fusion.7
  (331 shorter events, 292.6 us)
Async XLA Ops:
  11.4 30.5 %all-to-all-start.2 = ((bf16[64,4,1024]{2,1,0:T(4,128)(2,1)}), bf16[64,4,1024]{2,1,0:T(4,128)(2,1)S(1)}, u32[]{:S(2)}, u32[]{:S(2)}) async-start(bf16[64,4,1024]{2,1,0:T(4,128)(2,1)} %all_to_all.70), calls=%async_computation.2 | async-start | bytes 1048576 | tf_op jit(solution)/shard_map/all_to_all | solution.py:74
  41.9 23.6 %all-to-all-start = ((bf16[64,4,1024]{2,1,0:T(4,128)(2,1)}), bf16[64,4,1024]{2,1,0:T(4,128)(2,1)S(1)}, u32[]{:S(2)}, u32[]{:S(2)}) async-start(bf16[64,4,1024]{2,1,0:T(4,128)(2,1)} %all_to_all.64), calls=%async_computation | async-start | bytes 1048576 | tf_op jit(solution)/shard_map/all_to_all | solution.py:77
  48.2 199.1 %all-gather.5.cloned.1.call-start = ((), (), s32[]{:S(2)}) async-start(), calls=%async_computation.8 | async-start | bytes 34078720 | tf_op jit(solution)/shard_map/all_gather | solution.py:15
  70.5 28.4 %all-to-all-start.1 = ((bf16[64,4,1024]{2,1,0:T(4,128)(2,1)}), bf16[64,4,1024]{2,1,0:T(4,128)(2,1)S(1)}, u32[]{:S(2)}, u32[]{:S(2)}) async-start(bf16[64,4,1024]{2,1,0:T(4,128)(2,1)} %all_to_all.67), calls=%async_computation.1 | async-start | bytes 1048576 | tf_op jit(solution)/shard_map/all_to_all | solution.py:67
  98.9 145.8 %all-to-all-start.4 = ((bf16[64,4,1024]{2,1,0:T(4,128)(2,1)}), bf16[64,4,1024]{2,1,0:T(4,128)(2,1)S(1)}, u32[]{:S(2)}, u32[]{:S(2)}) async-start(bf16[64,4,1024]{2,1,0:T(4,128)(2,1)} %all_to_all.76), calls=%async_computation.4 | async-start | bytes 1048576 | tf_op jit(solution)/shard_map/all_to_all | solution.py:84
  105.1 480.4 %all-gather.7.cloned.1.call-start = ((), (), s32[]{:S(2)}) async-start(), calls=%async_computation.9 | async-start | bytes 34078720 | tf_op jit(solution)/shard_map/all_gather | solution.py:15
  440.6 167.8 %all-to-all-start.5 = ((bf16[64,4,1024]{2,1,0:T(4,128)(2,1)}), bf16[64,4,1024]{2,1,0:T(4,128)(2,1)}, u32[]{:S(2)}, u32[]{:S(2)}) async-start(bf16[64,4,1024]{2,1,0:T(4,128)(2,1)} %all_to_all.79), calls=%async_computation.5 | async-start | bytes 1048576 | tf_op jit(solution)/shard_map/all_to_all | solution.py:168
  608.4 181.7 %all-to-all-start.3 = ((bf16[64,4,1024]{2,1,0:T(4,128)(2,1)}), bf16[64,4,1024]{2,1,0:T(4,128)(2,1)S(1)}, u32[]{:S(2)}, u32[]{:S(2)}) async-start(bf16[64,4,1024]{2,1,0:T(4,128)(2,1)} %all_to_all.73), calls=%async_computation.3 | async-start | bytes 1048576 | tf_op jit(solution)/shard_map/all_to_all | solution.py:161
  790.1 27.7 %all-to-all-start.6 = ((bf16[64,4,1024]{2,1,0:T(4,128)(2,1)}), bf16[64,4,1024]{2,1,0:T(4,128)(2,1)S(1)}, u32[]{:S(2)}, u32[]{:S(2)}) async-start(bf16[64,4,1024]{2,1,0:T(4,128)(2,1)} %all_to_all.82), calls=%async_computation.6 | async-start | bytes 1048576 | tf_op jit(solution)/shard_map/all_to_all | solution.py:175
  817.8 23.6 %all-to-all-start.7 = ((bf16[64,4,1024]{2,1,0:T(4,128)(2,1)}), bf16[64,4,1024]{2,1,0:T(4,128)(2,1)S(1)}, u32[]{:S(2)}, u32[]{:S(2)}) async-start(bf16[64,4,1024]{2,1,0:T(4,128)(2,1)} %all_to_all.85), calls=%async_computation.7 | async-start | bytes 1048576 | tf_op jit(solution)/shard_map/all_to_all | solution.py:182
Sparse Core Ops, SparseCore 0:
  67.9 157.1 all-gather.4
  437.4 148.0 all-gather.6
where the time goes:
time: 858 us; the launch traced here: 850 us
  waiting for transfers between devices  202 us (24%)
  other arithmetic  193 us (22%)
  blocking collectives  149 us (17%)
  local copies, waits for them, and re-layouts  134 us (16%)
  loops' own time  85.1 us (10%)
  starting transfers between devices  63.3 us (7%)
  between operations  15.7 us (2%)
    select_n x126, other arithmetic, step(): jnp.where(position < mine, new, old)  187 us
    unnamed x1, blocking collectives  134 us
    all_gather x2, waiting for transfers between devices, carried_in(): pieces = jax.tree.map(lambda part: lax.all_gather(part, axis), value)  133 us
    another operation x2, loops' own time, carried_in(): return lax.fori_loop(0, count - 1, step, subtotal)  85.1 us
    dynamic_slice x126, local copies, waits for them, and re-layouts, step(): longer = join(subtotal, jax.tree.map(lambda part: part[position], pieces))  74 us
    rev x2, local copies, waits for them, and re-layouts, carried_in(): pieces = jax.tree.map(lambda part: part[::-1], pieces)  23.1 us
    all_to_all x1, waiting for transfers between devices, body(): lax.all_to_all(pack_rows(query_in, send_slot, slot_total), 'ctx', split_a...  19.3 us
  transfers between devices with their start and end apart: 10, of which 6 were waited for; matrix products, arithmetic and copies ran while one was open for 22% of the time, Pallas kernels for 0%

commit v1 on v0

--- a/solution.py
+++ b/solution.py
@@ -1,6 +1,9 @@
+import functools
 import jax
 import jax.numpy as jnp
 from jax import lax
+from jax.experimental import pallas as pl
+from jax.experimental.pallas import tpu as pltpu
 from jax.sharding import PartitionSpec as P
 
 HEAD_DIM = 128
@@ -45,7 +48,7 @@
     return (later_one[0] + (1.0 - later_one[1]) * earlier[0], jnp.maximum(earlier[1], later_one[1]))
 
 
-def body(query_in, key_in, value_in, out_grad, chain_order, load_order, doc_lengths):
+def general_body(query_in, key_in, value_in, out_grad, chain_order, load_order, doc_lengths):
     row_count, width_dev = query_in.shape
     heads_dev = width_dev // HEAD_DIM
     shards = lax.axis_size("ctx")
@@ -191,6 +194,595 @@
     return (attended, query_grad, key_grad, value_grad)
 
 
+SOURCES = 64
+GROUPS = 8
+MAIN = 16
+EXTRA = 4
+ROWS = 4 * (MAIN + EXTRA)
+MAIN_SLOTS = SOURCES * MAIN
+SLOTS = SOURCES * (MAIN + EXTRA)
+GROUP_TOKENS = 1024
+TILE = 128
+PART = 256
+TILES = SLOTS // TILE
+PARTS = SLOTS // PART
+TOKENS = 8192
+HEADS_HERE = 8
+MESH = pl.DeviceIdType.MESH
+F32 = jnp.float32
+LOW = jnp.bfloat16
+
+
+def nn(left, right, precision=None):
+    return lax.dot_general(
+        left, right, (((1,), (0,)), ((), ())), precision=precision, preferred_element_type=F32
+    )
+
+
+def nt(left, right, precision=None):
+    return lax.dot_general(
+        left, right, (((1,), (1,)), ((), ())), precision=precision, preferred_element_type=F32
+    )
+
+
+def tn(left, right):
+    return lax.dot_general(left, right, (((0,), (0,)), ((), ())), preferred_element_type=F32)
+
+
+def iota(shape, dim):
+    return lax.broadcasted_iota(jnp.int32, shape, dim)
+
+
+def turned(row):
+    return jnp.transpose(jnp.broadcast_to(row, (TILE, TILE)))
+
+
+def ones_where(mask):
+    return jnp.where(mask, 1.0, 0.0)
+
+
+def group_and_rank(chain_row, axis):
+    across = jnp.broadcast_to(chain_row, (TILE, TILE))
+    down = jnp.transpose(across)
+    group_across = jnp.floor(across * (1.0 / GROUP_TOKENS))
+    group_down = jnp.floor(down * (1.0 / GROUP_TOKENS))
+    same = group_across == group_down
+    if axis == 0:
+        rank = jnp.sum(ones_where(same & (down < across)), axis=0, keepdims=True)
+        return group_across[0:1], rank
+    rank = jnp.sum(ones_where(same & (across < down)), axis=1, keepdims=True)
+    return group_down[:, 0:1], rank
+
+
+def fused_kernel(
+    query_hbm,
+    key_hbm,
+    value_hbm,
+    grad_hbm,
+    chain_ref,
+    load_ref,
+    length_ref,
+    back_ref,
+    rows_in,
+    packed,
+    landed,
+    outgoing,
+    load_own,
+    load_all,
+    spread,
+    gathered,
+    pos_wide,
+    start_wide,
+    carry_wide,
+    onward_wide,
+    root_wide,
+    inner_wide,
+    row_facts,
+    queries,
+    keys,
+    values,
+    grads,
+    dgrads,
+    raw,
+    key_sum,
+    value_sum,
+    extra_out,
+    scores_turned,
+    state_own,
+    state_all,
+    back_own,
+    back_all,
+    stage_one,
+    stage_two,
+    in_sem,
+    load_sem,
+    data_send,
+    data_recv,
+    state_send,
+    state_recv,
+    sum_send,
+    sum_recv,
+    out_send,
+    out_recv,
+):
+    place, x = lax.axis_index("ctx"), lax.axis_index("head")
+    y, z, c = place // 16, lax.rem(place // 2, 8), lax.rem(place, 2)
+    mine = y * 2 + c
+
+    def at(j, zz):
+        yy, cc = lax.rem(y + j // 2, 4), lax.rem(c + lax.rem(j, 2), 2)
+        return (yy * 8 + zz) * 2 + cc, yy * 2 + cc
+
+    def remote(src, dst, send, recv, ctx, head):
+        return pltpu.make_async_remote_copy(
+            src_ref=src,
+            dst_ref=dst,
+            send_sem=send,
+            recv_sem=recv,
+            device_id=(ctx, head),
+            device_id_type=MESH,
+        )
+
+    def settle(ref, sem):
+        pltpu.make_async_copy(ref, ref, sem).wait()
+
+    inputs = (query_hbm, key_hbm, value_hbm, grad_hbm)
+    for a, source in enumerate(inputs):
+        pltpu.make_async_copy(source, rows_in.at[pl.ds(a * TILE, TILE)], in_sem.at[a]).start()
+
+    barrier = pltpu.get_barrier_semaphore()
+
+    def greet(i, carry):
+        ctx, unused = at(lax.rem(i, 8), lax.rem(z + i // 8, 8))
+        pl.semaphore_signal(barrier, inc=1, device_id=(ctx, x), device_id_type=MESH)
+        return carry
+
+    lax.fori_loop(1, 64, greet, 0)
+    for j in range(1, 4):
+        pl.semaphore_signal(
+            barrier, inc=1, device_id=(place, lax.rem(x + j, 4)), device_id_type=MESH
+        )
+
+    group, rank = group_and_rank(chain_ref[...].astype(F32), 0)
+    targets = []
+    for a in range(4):
+        main_row = (a * MAIN if a < 3 else 3 * MAIN + 4 * EXTRA) + rank
+        extra_row = 3 * MAIN + a * EXTRA + rank - MAIN
+        targets.append(group * ROWS + jnp.where(rank < MAIN, main_row, extra_row))
+    target = jnp.concatenate(targets, axis=1).astype(jnp.int32)
+    load_own[...] = jnp.broadcast_to(load_ref[...], (8, TILE))
+    for a, source in enumerate(inputs):
+        pltpu.make_async_copy(source, rows_in.at[pl.ds(a * TILE, TILE)], in_sem.at[a]).wait()
+    pl.semaphore_wait(barrier, 66)
+
+    owner = place // 8
+    for j in range(8):
+        ctx, unused = at(j, owner)
+        send = load_sem.at[1 if j == 0 else 0]
+        if j == 0:
+
+            @pl.when(owner == z)
+            def _():
+                pltpu.make_async_copy(
+                    load_own, load_all.at[lax.rem(place, 8)], load_sem.at[2]
+                ).start()
+
+            @pl.when(owner != z)
+            def _():
+                remote(
+                    load_own, load_all.at[lax.rem(place, 8)], send, load_sem.at[2], ctx, x
+                ).start()
+        else:
+            remote(load_own, load_all.at[lax.rem(place, 8)], send, load_sem.at[2], ctx, x).start()
+
+    early, late = pl.ds(0, 64), pl.ds(64, 16)
+    row_number = iota((ROWS, 4 * TILE), 0)
+
+    def send_rows(slot, ctx, rows, recv):
+        remote(
+            packed.at[slot, rows], landed.at[place, rows], data_send, data_recv.at[recv], ctx, x
+        ).start()
+
+    def keep_rows(slot, rows, recv):
+        pltpu.make_async_copy(
+            packed.at[slot, rows], landed.at[place, rows], data_recv.at[recv]
+        ).start()
+
+    def pack_group(i, carry):
+        goal = lax.rem(z + i + 1, 8)
+        pick = ones_where(row_number + goal * ROWS == target).astype(LOW)
+        block = nn(pick, rows_in[...]).astype(LOW)
+        for head in range(HEADS_HERE):
+            packed[goal * 8 + head] = block[:, head * TILE : (head + 1) * TILE]
+        for j in range(8):
+            ctx, head = at(j, goal)
+            if j == 0:
+
+                @pl.when(i < 7)
+                def _():
+                    send_rows(goal * 8 + head, ctx, early, 0)
+
+            else:
+                send_rows(goal * 8 + head, ctx, early, 0)
+        return carry
+
+    lax.fori_loop(0, 8, pack_group, 0)
+    keep_rows(z * 8 + mine, early, 0)
+    keep_rows(z * 8 + mine, late, 1)
+
+    def send_late(i, carry):
+        goal = lax.rem(z + i // 8, 8)
+        ctx, head = at(lax.rem(i, 8), goal)
+        send_rows(goal * 8 + head, ctx, late, 1)
+        return carry
+
+    lax.fori_loop(1, 64, send_late, 0)
+
+    down, across = iota((TILE, TILE), 0), iota((TILE, TILE), 1)
+    lengths = jnp.broadcast_to(length_ref[...].astype(F32), (TILE, TILE))
+    ends_down = jnp.sum(jnp.where(across <= down, lengths, 0.0), axis=1, keepdims=True)
+    ends = jnp.transpose(jnp.broadcast_to(ends_down, (TILE, TILE)))
+    base = (z * GROUP_TOKENS).astype(F32)
+    top = base + float(GROUP_TOKENS)
+
+    def goes_on(last_tokens, first):
+        start = jnp.max(
+            jnp.where(ends[0:1] <= last_tokens - 1.0, ends[0:1], 0.0), axis=1, keepdims=True
+        )
+        return ones_where(start < first)
+
+    def spreading(shape, first):
+        number, other = iota(shape, first), iota(shape, 1 - first)
+        array, rest = number // 256, lax.rem(number, 256)
+        goal = (rest // 4) * 16 + array * 4 + lax.rem(rest, 4)
+        return ones_where(goal == other).astype(LOW)
+
+    def fill_spread(i, carry):
+        number = iota((TILE, 1024), 0) + i * TILE
+        array, rest = number // 256, lax.rem(number, 256)
+        goal = (rest // 4) * 16 + array * 4 + lax.rem(rest, 4)
+        rows = pl.ds(pl.multiple_of(i * TILE, TILE), TILE)
+        gathered[rows] = ones_where(goal == iota((TILE, 1024), 1)).astype(LOW)
+        source, rest = number // 16, lax.rem(number, 16)
+        origin = (rest // 4) * 256 + source * 4 + lax.rem(rest, 4)
+        spread[rows] = ones_where(origin == iota((TILE, 1024), 1)).astype(LOW)
+        return carry
+
+    lax.fori_loop(0, 8, fill_spread, 0)
+
+    settle(load_all, load_sem.at[2])
+    below = ones_where(across < down).astype(LOW)
+    slot_number = iota((TILE, SLOTS), 1).astype(F32)
+    fact_row, fact_lane = iota((8, TILE), 0), iota((8, TILE), 1)
+    seen = jnp.zeros((1, TILE), F32)
+    facts = jnp.zeros((8, SLOTS), F32)
+    for j in range(8):
+        source = (load_all[j, 0:1] // TILE).astype(F32)
+        source_wide = turned(source)
+        same = ones_where(source_wide == across.astype(F32))
+        earlier = nn(below, same.astype(LOW)) + seen
+        place_in = jnp.sum(same * earlier, axis=1, keepdims=True)
+        seen = seen + jnp.sum(same, axis=0, keepdims=True)
+        source_column = source_wide[:, 0:1]
+        slot = jnp.where(
+            place_in < MAIN,
+            source_column * MAIN + place_in,
+            MAIN_SLOTS + source_column * EXTRA + place_in - MAIN,
+        )
+        pick = ones_where(slot == slot_number).astype(LOW)
+        told = jnp.where(
+            fact_row == 0, j, jnp.where(fact_row == 1, fact_lane, jnp.where(fact_row == 2, 1, 0))
+        )
+        facts = facts + nn(told.astype(F32).astype(LOW), pick)
+    position = jnp.where(facts[2:3] > 0.5, base + facts[0:1] * TILE + facts[1:2], -1.0)
+    row_facts[0:1] = position
+    for t in range(TILES):
+        tile = slice(t * TILE, (t + 1) * TILE)
+        where = turned(position[:, tile])
+        start = jnp.max(jnp.where(ends <= where, ends, 0.0), axis=1, keepdims=True)
+        end = jnp.min(jnp.where(ends > where, ends, float(TOKENS)), axis=1, keepdims=True)
+        start_all = jnp.broadcast_to(start, (TILE, TILE))
+        pos_wide[tile] = where
+        start_wide[tile] = start_all
+        carry_wide[tile] = ones_where((start_all < base) & (where >= 0.0))
+        onward_wide[tile] = ones_where((jnp.broadcast_to(end, (TILE, TILE)) > top) & (where >= 0.0))
+        row_facts[1:2, tile] = jnp.transpose(start_all)[0:1]
+
+    def part(i):
+        return pl.ds(pl.multiple_of(i * PART, PART), PART)
+
+    settle(landed.at[:, early], data_recv.at[0])
+    extra = nn(gathered[...], landed[:, 48:64].reshape(1024, TILE)).astype(LOW)
+    for a, ref in enumerate((queries, keys, values)):
+        ref[0:MAIN_SLOTS] = landed[:, a * MAIN : (a + 1) * MAIN].reshape(MAIN_SLOTS, TILE)
+        ref[MAIN_SLOTS:SLOTS] = extra[a * 256 : (a + 1) * 256]
+    grads[MAIN_SLOTS:SLOTS] = extra[768:1024]
+
+    kept = (keys[...].astype(F32) * onward_wide[...]).astype(LOW)
+    state_own[...] = tn(kept, values[...])
+    for n in (1, 2):
+        ctx, unused = at(0, lax.rem(z + n, 8))
+        remote(
+            state_own, state_all.at[n - 1], state_send.at[0], state_recv.at[n - 1], ctx, x
+        ).start()
+
+    def forward_part(i, carry):
+        rows = part(i)
+        where, start = pos_wide[rows][:, 0:1], start_wide[rows][:, 0:1]
+        inside = (row_facts[0:1] <= where) & (row_facts[0:1] >= start)
+        scores = nt(queries[rows], keys[...])
+        low = jnp.where(inside, scores, 0.0).astype(LOW)
+        raw[rows] = nn(low, values[...])
+        return carry
+
+    lax.fori_loop(0, PARTS, forward_part, 0)
+    settle(state_all.at[0], state_recv.at[0])
+    settle(state_all.at[1], state_recv.at[1])
+    state = state_all[0] + goes_on(base, base - float(GROUP_TOKENS)) * state_all[1]
+    state_low = state.astype(LOW)
+    raw[...] = raw[...] + carry_wide[...] * nn(queries[...], state_low)
+
+    def tile_sums(product):
+        row = iota((16, TILE), 0)
+        total = jnp.zeros((16, TILE), F32)
+        ones = jnp.ones((16, TILE), F32)
+        for t in range(TILES):
+            tile = product(slice(t * TILE, (t + 1) * TILE))
+            total = jnp.where(row == t, nt(ones, tile, lax.Precision.HIGHEST), total)
+        return total
+
+    def head_sum_start(k, partial):
+        stage_one[k, mine] = partial
+        for j in range(1, 8):
+            ctx, unused = at(j, z)
+            remote(
+                stage_one.at[k, mine],
+                stage_one.at[k, mine],
+                sum_send.at[2 * k],
+                sum_recv.at[2 * k],
+                ctx,
+                x,
+            ).start()
+
+    def head_sum_next(k):
+        settle(stage_one.at[k, pl.ds(0, 7)], sum_recv.at[2 * k])
+        total = stage_one[k, 0]
+        for j in range(1, 8):
+            total = total + stage_one[k, j]
+        stage_two[k, x] = total
+        for j in range(1, 4):
+            remote(
+                stage_two.at[k, x],
+                stage_two.at[k, x],
+                sum_send.at[2 * k + 1],
+                sum_recv.at[2 * k + 1],
+                place,
+                lax.rem(x + j, 4),
+            ).start()
+
+    def head_sum_end(k):
+        settle(stage_two.at[k, pl.ds(0, 3)], sum_recv.at[2 * k + 1])
+        return (stage_two[k, 0] + stage_two[k, 1]) + (stage_two[k, 2] + stage_two[k, 3])
+
+    head_sum_start(0, tile_sums(lambda tile: raw[tile] * raw[tile]))
+
+    def turned_part(i, carry):
+        rows = part(i)
+        where = pos_wide[rows][:, 0:1]
+        inside = (where <= row_facts[0:1]) & (where >= row_facts[1:2])
+        scores = nt(keys[rows], queries[...])
+        scores_turned[rows] = jnp.where(inside, scores, 0.0).astype(LOW)
+        return carry
+
+    lax.fori_loop(0, PARTS, turned_part, 0)
+    head_sum_next(0)
+    settle(landed.at[:, late], data_recv.at[1])
+    grads[0:MAIN_SLOTS] = landed[:, 64:80].reshape(MAIN_SLOTS, TILE)
+    head_sum_start(1, tile_sums(lambda tile: raw[tile] * grads[tile].astype(F32)))
+    total = head_sum_end(0)
+    inverse = 1.0 / jnp.sqrt(total / FEATURES + epsilon)
+    for t in range(TILES):
+        root_wide[t * TILE : (t + 1) * TILE] = turned(inverse[t : t + 1])
+    raw[...] = raw[...] * root_wide[...]
+    attended = raw[...].astype(LOW)
+    outgoing[:, 0:MAIN] = attended[0:MAIN_SLOTS].reshape(SOURCES, MAIN, TILE)
+    extra_out[0:256] = attended[MAIN_SLOTS:SLOTS]
+    head_sum_next(1)
+
+    def send_back(rows):
+        def one(i, carry):
+            ctx, unused = at(lax.rem(i, 8), lax.rem(z + i // 8, 8))
+            remote(
+                outgoing.at[ctx, rows], back_ref.at[z, mine, rows], out_send, out_recv, ctx, x
+            ).start()
+            return carry
+
+        lax.fori_loop(1, 64, one, 0)
+        pltpu.make_async_copy(
+            outgoing.at[place, rows], back_ref.at[z, mine, rows], out_recv
+        ).start()
+
+    send_back(pl.ds(0, MAIN))
+    inner = head_sum_end(1) * inverse / FEATURES
+    for t in range(TILES):
+        inner_wide[t * TILE : (t + 1) * TILE] = turned(inner[t : t + 1])
+    dgrads[...] = (
+        (grads[...].astype(F32) - raw[...] * inner_wide[...]) * root_wide[...]
+    ).astype(LOW)
+
+    kept_queries = (queries[...].astype(F32) * carry_wide[...]).astype(LOW)
+    back_own[...] = tn(kept_queries, dgrads[...])
+    for n in (1, 2):
+        ctx, unused = at(0, lax.rem(z + 8 - n, 8))
+        remote(
+            back_own, back_all.at[n - 1], state_send.at[1], state_recv.at[n + 1], ctx, x
+        ).start()
+
+    for i in range(PARTS):
+        rows = slice(i * PART, (i + 1) * PART)
+        where, start = pos_wide[rows, 0:1], start_wide[rows, 0:1]
+        inside = (row_facts[0:1] <= where) & (row_facts[0:1] >= start)
+        mixed = jnp.where(inside, nt(dgrads[rows], values[...]), 0.0).astype(LOW)
+        query_part = nn(mixed, keys[...]) + carry_wide[rows] * nt(dgrads[rows], state_low)
+        query_low = query_part.astype(LOW)
+        if i < MAIN_SLOTS // PART:
+            outgoing[i * 16 : (i + 1) * 16, MAIN : 2 * MAIN] = query_low.reshape(16, MAIN, TILE)
+        else:
+            extra_out[256:512] = query_low
+    send_back(pl.ds(MAIN, MAIN))
+
+    def key_value_part(i, carry):
+        rows = part(i)
+        where = pos_wide[rows][:, 0:1]
+        inside = (where <= row_facts[0:1]) & (where >= row_facts[1:2])
+        mixed = jnp.where(inside, nt(values[rows], dgrads[...]), 0.0).astype(LOW)
+        key_sum[rows] = nn(mixed, queries[...])
+        value_sum[rows] = nn(scores_turned[rows], dgrads[...])
+        return carry
+
+    lax.fori_loop(0, PARTS, key_value_part, 0)
+    settle(back_all.at[0], state_recv.at[2])
+    settle(back_all.at[1], state_recv.at[3])
+    back = back_all[0] + goes_on(top + float(GROUP_TOKENS), top) * back_all[1]
+    back_low = back.astype(LOW)
+    key_low = (key_sum[...] + onward_wide[...] * nt(values[...], back_low)).astype(LOW)
+    value_low = (value_sum[...] + onward_wide[...] * nn(keys[...], back_low)).astype(LOW)
+    outgoing[:, 2 * MAIN : 3 * MAIN] = key_low[0:MAIN_SLOTS].reshape(SOURCES, MAIN, TILE)
+    outgoing[:, 3 * MAIN : 4 * MAIN] = value_low[0:MAIN_SLOTS].reshape(SOURCES, MAIN, TILE)
+    extra_out[512:768] = key_low[MAIN_SLOTS:SLOTS]
+    extra_out[768:1024] = value_low[MAIN_SLOTS:SLOTS]
+    extra_rows = nn(spread[...], extra_out[...]).astype(LOW)
+    outgoing[:, 4 * MAIN : ROWS] = extra_rows.reshape(SOURCES, 4 * EXTRA, TILE)
+    send_back(pl.ds(2 * MAIN, 3 * MAIN))
+
+    settle(load_all.at[pl.ds(0, 7)], load_sem.at[0])
+
+    @pl.when(owner != z)
+    def _():
+        settle(load_own, load_sem.at[1])
+
+    settle(packed.at[pl.ds(0, 63)], data_send)
+    settle(state_all, state_send.at[0])
+    settle(back_all, state_send.at[1])
+    for k in range(2):
+        settle(stage_one.at[k, pl.ds(0, 7)], sum_send.at[2 * k])
+        settle(stage_two.at[k, pl.ds(0, 3)], sum_send.at[2 * k + 1])
+    settle(outgoing.at[pl.ds(0, 63)], out_send)
+    settle(outgoing, out_recv)
+
+
+def unpack_kernel(chain_ref, back_ref, attended_ref, query_ref, key_ref, value_ref):
+    group, rank = group_and_rank(chain_ref[...].astype(F32), 1)
+    number = iota((TILE, GROUPS * ROWS), 1).astype(F32)
+    picks = []
+    for a in range(4):
+        row = jnp.where(rank < MAIN, a * MAIN + rank, 4 * MAIN + a * EXTRA + rank - MAIN)
+        picks.append(ones_where(group * ROWS + row == number).astype(LOW))
+    pick = jnp.concatenate(picks, axis=0)
+    for head in range(HEADS_HERE):
+        found = nn(pick, back_ref[:, head].reshape(GROUPS * ROWS, TILE)).astype(LOW)
+        lanes = slice(head * TILE, (head + 1) * TILE)
+        for a, ref in enumerate((attended_ref, query_ref, key_ref, value_ref)):
+            ref[:, lanes] = found[a * TILE : (a + 1) * TILE]
+
+
+def fast_body(query_in, key_in, value_in, out_grad, chain_order, load_order, doc_lengths):
+    chain_row = chain_order.reshape(1, TILE)
+    whole = pl.BlockSpec(memory_space=pltpu.VMEM)
+    anywhere = pl.BlockSpec(memory_space=pl.ANY)
+    wide = pltpu.VMEM((SLOTS, TILE), F32)
+    low = pltpu.VMEM((SLOTS, TILE), LOW)
+    dma = pltpu.SemaphoreType.DMA
+    returned = pl.pallas_call(
+        fused_kernel,
+        out_shape=jax.ShapeDtypeStruct((GROUPS, HEADS_HERE, ROWS, TILE), LOW),
+        in_specs=[anywhere] * 4 + [whole] * 3,
+        out_specs=anywhere,
+        scratch_shapes=[
+            pltpu.VMEM((4 * TILE, HEADS_HERE * TILE), LOW),
+            pltpu.VMEM((SOURCES, ROWS, TILE), LOW),
+            pltpu.VMEM((SOURCES, ROWS, TILE), LOW),
+            pltpu.VMEM((SOURCES, ROWS, TILE), LOW),
+            pltpu.VMEM((8, TILE), jnp.int32),
+            pltpu.VMEM((8, 8, TILE), jnp.int32),
+            pltpu.VMEM((1024, 1024), LOW),
+            pltpu.VMEM((1024, 1024), LOW),
+            wide,
+            wide,
+            wide,
+            wide,
+            wide,
+            wide,
+            pltpu.VMEM((8, SLOTS), F32),
+            low,
+            low,
+            low,
+            low,
+            low,
+            wide,
+            wide,
+            wide,
+            pltpu.VMEM((1024, TILE), LOW),
+            pltpu.VMEM((SLOTS, SLOTS), LOW),
+            pltpu.VMEM((TILE, TILE), F32),
+            pltpu.VMEM((2, TILE, TILE), F32),
+            pltpu.VMEM((TILE, TILE), F32),
+            pltpu.VMEM((2, TILE, TILE), F32),
+            pltpu.VMEM((2, 8, 16, TILE), F32),
+            pltpu.VMEM((2, 4, 16, TILE), F32),
+            dma((4,)),
+            dma((3,)),
+            dma,
+            dma((2,)),
+            dma((2,)),
+            dma((4,)),
+            dma((4,)),
+            dma((4,)),
+            dma,
+            dma,
+        ],
+        compiler_params=pltpu.CompilerParams(
+            collective_id=0, has_side_effects=True, vmem_limit_bytes=48 << 20
+        ),
+        name="fused",
+    )(
+        query_in,
+        key_in,
+        value_in,
+        out_grad,
+        chain_row,
+        load_order.reshape(1, TILE),
+        doc_lengths.reshape(1, TILE),
+    )
+    out = jax.ShapeDtypeStruct((TILE, HEADS_HERE * TILE), LOW)
+    return pl.pallas_call(
+        unpack_kernel,
+        out_shape=(out,) * 4,
+        in_specs=[whole] * 2,
+        out_specs=(whole,) * 4,
+        compiler_params=pltpu.CompilerParams(vmem_limit_bytes=32 << 20),
+        name="unpack",
+    )(chain_row, returned)
+
+
+def body(query_in, key_in, value_in, out_grad, chain_order, load_order, doc_lengths):
+    ahead = jnp.mod(chain_order // TILE - lax.axis_index("ctx"), SOURCES)
+    windows = jnp.mod(ahead[None, :] - jnp.arange(SOURCES)[:, None], SOURCES) < GROUPS
+    most = jnp.max(jnp.sum(windows.astype(jnp.int32), axis=1))
+    return lax.cond(
+        most <= MAIN + EXTRA,
+        fast_body,
+        general_body,
+        query_in,
+        key_in,
+        value_in,
+        out_grad,
+        chain_order,
+        load_order,
+        doc_lengths,
+    )
+
+
 def solution(mesh):
     return jax.shard_map(
         body,

time: 858 us -> 114 us (0.13)
  waiting for transfers between devices: 202 us -> 0 us
  other arithmetic: 193 us -> 1.44 us
  blocking collectives: 149 us -> 0 us
  local copies, waits for them, and re-layouts: 134 us -> 0 us
  Pallas kernels: 0 us -> 97.6 us
  loops' own time: 85.1 us -> 0.17 us
  starting transfers between devices: 63.3 us -> 0 us
    select_n x130 -> x1, other arithmetic: 189 us -> 0.67 us  [body(): ahead = jnp.mod(chain_order // TILE - lax.axis_index('ctx'), SOURCES)]
    unnamed x1 -> x0, blocking collectives: 134 us -> none
    all_gather x2 -> x0, waiting for transfers between devices: 133 us -> none  [carried_in(): pieces = jax.tree.map(lambda part: lax.all_gather(part, axis), value)]
    pallas_call x0 -> x2, Pallas kernels: none -> 97.6 us  [the longest x1 94.3 us: fast_body(): pl.pallas_call(fused_kernel, out_shape=jax.ShapeDtypeStruct((GROUPS, HEAD...]
    another operation x2 -> x1, loops' own time: 85.1 us -> 0.17 us  [body(): lax.cond(most <= MAIN + EXTRA, fast_body, general_body, query_in, key_in,...]
    dynamic_slice x126 -> x0, local copies, waits for them, and re-layouts: 74 us -> none  [step(): longer = join(subtotal, jax.tree.map(lambda part: part[position], pieces))]
    all_to_all x8 -> x0, waiting for transfers between devices: 69.2 us -> none  [the longest x1 19.3 us: body(): lax.all_to_all(pack_rows(query_in, send_slot, slot_total), 'ctx', split_a...]
    all_to_all x8 -> x0, starting transfers between devices: 63.2 us -> none  [the longest x1 13.2 us: body(): lax.all_to_all(pack_rows(key_in, send_slot, slot_total), 'ctx', split_axi...]
  transfers between devices with their start and end apart: 10 -> 0, of which waited for: 6 -> 0; matrix products, arithmetic and copies ran while one was open for 22% -> 0% of each run, Pallas kernels for 0% -> 0%
where the time goes in v1:
time: 114 us
  Pallas kernels  97.6 us (86%)
  between operations  14.7 us (13%)
  other arithmetic  1.44 us (1%)
    pallas_call x1, Pallas kernels, fast_body(): pl.pallas_call(fused_kernel, out_shape=jax.ShapeDtypeStruct((GROUPS, HEAD...  94.3 us
    pallas_call x1, Pallas kernels, fast_body(): pl.pallas_call(unpack_kernel, out_shape=(out,) * 4, in_specs=[whole] * 2,...  3.31 us

profile of v1, /device:TPU:1, one launch (start us, length us, event | category | flops | bytes accessed | tf_op | source)
XLA Modules:
  0.0 113.8 jit_solution(14001945465667671493)
XLA Ops:
  7.2 0.7 and_select_fusion.2
  7.8 0.1 convert_reduce_fusion.3
  8.0 0.6 reduce_max.9
  9.3 97.7 %conditional.1 = ((bf16[128,1024]{1,0:T(8,128)(2,1)}, bf16[128,1024]{1,0:T(8,128)(2,1)}, bf16[128,1024]{1,0:T(8,128)(2,1)}, bf16[128,1024]{1,0:T(8,128)(2,1)})) conditional(s32[]{:T(128)} %convert_element_type.86, (s32[128]{0:T(128)}, s32[128]{0:T(128)}, bf16[128,1024]{1,0:T(8,128)(2,1)}, bf16[128,1024]{1,0:T(8,128)(2,1)}, ...), branch_computations={%region_2.24_spmd, %region_24.25_spmd} | conditional | flops 408334528 | bytes 335259392 | solution.py:772
  9.4 94.3 %fused.1.back_ref = bf16[8,8,80,128]{3,2,1,0:T(8,128)(2,1)S(1)} custom-call(bf16[128,1024]{1,0:T(8,128)(2,1)} %get-tuple-element.227.query_hbm, bf16[128,1024]{1,0:T(8,128)(2,1)} %get-tuple-element.228.key_hbm, bf16[128,1024]{1,0:T(8,128)(2,1)} %get-tuple-element.229.value_hbm, bf16[128,1024]{1,0:T(8,128)(2,1)} %get-tuple-element.230.grad_hbm, ...), custom_call_target="tpu_custom_call" | custom-call | tf_op jit(solution)/shard_map/cond/branch_1_fun/fused/pallas_call | solution.py:696
  103.7 3.3 %unpack.1 = (bf16[128,1024]{1,0:T(8,128)(2,1)}, bf16[128,1024]{1,0:T(8,128)(2,1)}, bf16[128,1024]{1,0:T(8,128)(2,1)}, bf16[128,1024]{1,0:T(8,128)(2,1)}) custom-call(s32[1,128]{1,0:T(1,128)} %bitcast.112, bf16[8,8,80,128]{3,2,1,0:T(8,128)(2,1)S(1)} %fused.1.back_ref), custom_call_target="tpu_custom_call" | custom-call | tf_op jit(solution)/shard_map/cond/branch_1_fun/unpack/pallas_call | solution.py:758

commit v2 on v1

v2 whole, which is shorter than its diff:
```python
import functools
import jax
import jax.numpy as jnp
from jax import lax
from jax.experimental import pallas as pl
from jax.experimental.pallas import tpu as pltpu
from jax.sharding import PartitionSpec as P

HEAD_DIM = 128
FEATURES = 4096

epsilon = 1e-06

SOURCES = 64
GROUPS = 8
GROUP_TOKENS = 1024
TILE = 128
PART = 256
TOKENS = 8192
HEADS_HERE = 8
SMALL = (16, 4)
LARGE = (32, 0)
MESH = pl.DeviceIdType.MESH
F32 = jnp.float32
LOW = jnp.bfloat16


def nn(left, right, precision=None):
    return lax.dot_general(
        left, right, (((1,), (0,)), ((), ())), precision=precision, preferred_element_type=F32
    )


def nt(left, right, precision=None):
    return lax.dot_general(
        left, right, (((1,), (1,)), ((), ())), precision=precision, preferred_element_type=F32
    )


def tn(left, right):
    return lax.dot_general(left, right, (((0,), (0,)), ((), ())), preferred_element_type=F32)


def iota(shape, dim):
    return lax.broadcasted_iota(jnp.int32, shape, dim)


def turned(row):
    return jnp.transpose(jnp.broadcast_to(row, (TILE, TILE)))


def ones_where(mask):
    return jnp.where(mask, 1.0, 0.0)


def group_and_rank(chain_row, axis):
    across = jnp.broadcast_to(chain_row, (TILE, TILE))
    down = jnp.transpose(across)
    group_across = jnp.floor(across * (1.0 / GROUP_TOKENS))
    group_down = jnp.floor(down * (1.0 / GROUP_TOKENS))
    same = group_across == group_down
    if axis == 0:
        rank = jnp.sum(ones_where(same & (down < across)), axis=0, keepdims=True)
        return group_across[0:1], rank
    rank = jnp.sum(ones_where(same & (across < down)), axis=1, keepdims=True)
    return group_down[:, 0:1], rank


def fused_kernel(
    sizes,
    query_hbm,
    key_hbm,
    value_hbm,
    grad_hbm,
    chain_ref,
    load_ref,
    length_ref,
    back_ref,
    rows_in,
    packed,
    landed,
    outgoing,
    load_own,
    load_all,
    spread,
    gathered,
    carry_low,
    onward_low,
    inside,
    inside_turned,
    root_wide,
    inner_wide,
    row_facts,
    queries,
    kept_queries,
    keys,
    kept_keys,
    values,
    kept_values,
    grads,
    dgrads,
    raw,
    extra_out,
    scores_turned,
    state_own,
    state_all,
    back_own,
    back_all,
    stage_one,
    stage_two,
    in_sem,
    load_sem,
    data_send,
    data_recv,
    state_send,
    state_recv,
    sum_send,
    sum_recv,
    out_send,
    out_recv,
):
    main, extra = sizes
    rows_all = 4 * (main + extra)
    main_slots = SOURCES * main
    slots = main_slots + SOURCES * extra
    tiles, parts = slots // TILE, slots // PART
    early, late = pl.ds(0, 3 * main + 4 * extra), pl.ds(3 * main + 4 * extra, main)
    place, x = lax.axis_index("ctx"), lax.axis_index("head")
    y, z, c = place // 16, lax.rem(place // 2, 8), lax.rem(place, 2)
    mine = y * 2 + c

    def wrapped(value, size):
        return jnp.where(value >= size, value - size, value)

    rows_y = [wrapped(y + n, 4) for n in range(4)]
    plane = []
    for j in range(8):
        cc = c if j % 2 == 0 else 1 - c
        plane.append((rows_y[j // 2] * 16 + cc, rows_y[j // 2] * 2 + cc))

    def at(j, zz):
        return plane[j][0] + 2 * zz, plane[j][1]

    def each_other(act):
        for j in range(1, 8):
            act(*at(j, z), z)

        def level(i, carry):
            zz = wrapped(z + i, 8)
            for j in range(8):
                act(*at(j, zz), zz)
            return carry

        lax.fori_loop(1, 8, level, 0)

    def remote(src, dst, send, recv, ctx, head):
        return pltpu.make_async_remote_copy(
            src_ref=src,
            dst_ref=dst,
            send_sem=send,
            recv_sem=recv,
            device_id=(ctx, head),
            device_id_type=MESH,
        )

    def settle(ref, sem):
        pltpu.make_async_copy(ref, ref, sem).wait()

    inputs = (query_hbm, key_hbm, value_hbm, grad_hbm)
    for a, source in enumerate(inputs):
        pltpu.make_async_copy(source, rows_in.at[pl.ds(a * TILE, TILE)], in_sem.at[a]).start()

    barrier = pltpu.get_barrier_semaphore()

    def greet(ctx, head, zz):
        pl.semaphore_signal(barrier, inc=1, device_id=(ctx, x), device_id_type=MESH)

    each_other(greet)
    for j in range(1, 4):
        pl.semaphore_signal(
            barrier, inc=1, device_id=(place, wrapped(x + j, 4)), device_id_type=MESH
        )

    group, rank = group_and_rank(chain_ref[...].astype(F32), 0)
    targets = []
    for a in range(4):
        main_row = (a * main if a < 3 else 3 * main + 4 * extra) + rank
        extra_row = 3 * main + a * extra + rank - main
        targets.append(group * rows_all + jnp.where(rank < main, main_row, extra_row))
    target = jnp.concatenate(targets, axis=1).astype(jnp.int32)
    load_own[...] = jnp.broadcast_to(load_ref[...], (8, TILE))
    for a, source in enumerate(inputs):
        pltpu.make_async_copy(source, rows_in.at[pl.ds(a * TILE, TILE)], in_sem.at[a]).wait()
    pl.semaphore_wait(barrier, 66)

    owner = place // 8
    for j in range(8):
        ctx, unused = at(j, owner)
        send = load_sem.at[1 if j == 0 else 0]
        if j == 0:

            @pl.when(owner == z)
            def _():
                pltpu.make_async_copy(
                    load_own, load_all.at[lax.rem(place, 8)], load_sem.at[2]
                ).start()

            @pl.when(owner != z)
            def _():
                remote(
                    load_own, load_all.at[lax.rem(place, 8)], send, load_sem.at[2], ctx, x
                ).start()
        else:
            remote(load_own, load_all.at[lax.rem(place, 8)], send, load_sem.at[2], ctx, x).start()

    row_number = iota((rows_all, 4 * TILE), 0)

    def send_rows(slot, ctx, rows, recv):
        remote(
            packed.at[slot, rows], landed.at[place, rows], data_send, data_recv.at[recv], ctx, x
        ).start()

    def keep_rows(slot, rows, recv):
        pltpu.make_async_copy(
            packed.at[slot, rows], landed.at[place, rows], data_recv.at[recv]
        ).start()

    def pack_group(i, carry):
        goal = wrapped(z + i + 1, 8)
        pick = ones_where(row_number + goal * rows_all == target).astype(LOW)
        block = nn(pick, rows_in[...]).astype(LOW)
        for head in range(HEADS_HERE):
            packed[goal * 8 + head] = block[:, head * TILE : (head + 1) * TILE]
        for j in range(8):
            ctx, head = at(j, goal)
            if j == 0:

                @pl.when(i < 7)
                def _():
                    send_rows(goal * 8 + head, ctx, early, 0)

            else:
                send_rows(goal * 8 + head, ctx, early, 0)
        return carry

    lax.fori_loop(0, 8, pack_group, 0)
    keep_rows(z * 8 + mine, early, 0)
    keep_rows(z * 8 + mine, late, 1)

    def send_late(ctx, head, zz):
        send_rows(zz * 8 + head, ctx, late, 1)

    each_other(send_late)

    down, across = iota((TILE, TILE), 0), iota((TILE, TILE), 1)
    lengths = jnp.broadcast_to(length_ref[...].astype(F32), (TILE, TILE))
    ends_down = jnp.sum(jnp.where(across <= down, lengths, 0.0), axis=1, keepdims=True)
    ends = jnp.transpose(jnp.broadcast_to(ends_down, (TILE, TILE)))
    base = (z * GROUP_TOKENS).astype(F32)
    top = base + float(GROUP_TOKENS)

    def goes_on(last_tokens, first):
        start = jnp.max(
            jnp.where(ends[0:1] <= last_tokens - 1.0, ends[0:1], 0.0), axis=1, keepdims=True
        )
        return ones_where(start < first)

    if extra:
        number, other = iota((PART, PART), 0), iota((PART, PART), 1)
        array, rest = number // 64, lax.rem(number, 64)
        goal = (rest // 4) * 16 + array * 4 + lax.rem(rest, 4)
        gathered[...] = ones_where(goal == other).astype(LOW)
        source, rest = number // 16, lax.rem(number, 16)
        origin = (rest // 4) * 64 + source * 4 + lax.rem(rest, 4)
        spread[...] = ones_where(origin == other).astype(LOW)

    settle(load_all, load_sem.at[2])
    below = ones_where(across < down).astype(LOW)
    slot_number = iota((TILE, slots), 1).astype(F32)
    fact_row, fact_lane = iota((8, TILE), 0), iota((8, TILE), 1)
    seen = jnp.zeros((1, TILE), F32)
    facts = jnp.zeros((8, slots), F32)
    for j in range(8):
        source = (load_all[j, 0:1] // TILE).astype(F32)
        source_wide = turned(source)
        same = ones_where(source_wide == across.astype(F32))
        earlier = nn(below, same.astype(LOW)) + seen
        place_in = jnp.sum(same * earlier, axis=1, keepdims=True)
        seen = seen + jnp.sum(same, axis=0, keepdims=True)
        source_column = source_wide[:, 0:1]
        slot = jnp.where(
            place_in < main,
            source_column * main + place_in,
            main_slots + source_column * extra + place_in - main,
        )
        pick = ones_where(slot == slot_number).astype(LOW)
        told = jnp.where(
            fact_row == 0, j, jnp.where(fact_row == 1, fact_lane, jnp.where(fact_row == 2, 1, 0))
        )
        facts = facts + nn(told.astype(F32).astype(LOW), pick)
    position = jnp.where(facts[2:3] > 0.5, base + facts[0:1] * TILE + facts[1:2], -1.0)
    row_facts[0:1] = position
    for t in range(tiles):
        tile = slice(t * TILE, (t + 1) * TILE)
        where = turned(position[:, tile])
        start = jnp.max(jnp.where(ends <= where, ends, 0.0), axis=1, keepdims=True)
        end = jnp.min(jnp.where(ends > where, ends, float(TOKENS)), axis=1, keepdims=True)
        start_all = jnp.broadcast_to(start, (TILE, TILE))
        end_all = jnp.broadcast_to(end, (TILE, TILE))
        carry_low[tile] = ones_where((start_all < base) & (where >= 0.0)).astype(LOW)
        onward_low[tile] = ones_where((end_all > top) & (where >= 0.0)).astype(LOW)
        reached = (position <= where[:, 0:1]) & (position >= start)
        inside[tile] = ones_where(reached).astype(LOW)
        row_facts[1:2, tile] = jnp.transpose(start_all)[0:1]
    for t in range(tiles):
        tile = slice(t * TILE, (t + 1) * TILE)
        where = turned(position[:, tile])[:, 0:1]
        reaching = (where <= position) & (where >= row_facts[1:2])
        inside_turned[tile] = ones_where(reaching).astype(LOW)

    def part(i):
        return pl.ds(pl.multiple_of(i * PART, PART), PART)

    settle(landed.at[:, early], data_recv.at[0])
    for a, ref in enumerate((queries, keys, values)):
        ref[0:main_slots] = landed[:, a * main : (a + 1) * main].reshape(main_slots, TILE)
    if extra:
        held = landed[:, 3 * main : 3 * main + 4 * extra].reshape(1024, TILE)
        side = jnp.concatenate([held[n * PART : (n + 1) * PART] for n in range(4)], axis=1)
        sorted_rows = nn(gathered[...], side).astype(LOW)
        for n in range(4):
            for a, ref in enumerate((queries, keys, values, grads)):
                ref[main_slots + n * 64 : main_slots + (n + 1) * 64] = sorted_rows[
                    a * 64 : (a + 1) * 64, n * TILE : (n + 1) * TILE
                ]

    kept_keys[...] = keys[...] * onward_low[...]
    state_own[...] = tn(kept_keys[...], values[...])
    for n in (1, 2):
        ctx, unused = at(0, wrapped(z + n, 8))
        remote(
            state_own, state_all.at[n - 1], state_send.at[0], state_recv.at[n - 1], ctx, x
        ).start()
    kept_queries[...] = queries[...] * carry_low[...]
    kept_values[...] = values[...] * onward_low[...]

    def forward_part(i, carry):
        rows = part(i)
        low = nt(queries[rows], keys[...]).astype(LOW) * inside[rows]
        raw[rows] = nn(low, values[...])
        return carry

    lax.fori_loop(0, parts, forward_part, 0)
    settle(state_all.at[0], state_recv.at[0])
    settle(state_all.at[1], state_recv.at[1])
    state = state_all[0] + goes_on(base, base - float(GROUP_TOKENS)) * state_all[1]
    state_low = state.astype(LOW)
    raw[...] = raw[...] + nn(kept_queries[...], state_low)

    def tile_sums(product):
        row = iota((16, TILE), 0)
        total = jnp.zeros((16, TILE), F32)
        ones = jnp.ones((16, TILE), LOW)
        for t in range(tiles):
            tile = product(slice(t * TILE, (t + 1) * TILE))
            high = tile.astype(LOW)
            rest = (tile - high.astype(F32)).astype(LOW)
            total = jnp.where(row == t, nt(ones, high) + nt(ones, rest), total)
        return total

    def head_sum_start(k, partial):
        stage_one[k, mine] = partial
        for j in range(1, 8):
            ctx, unused = at(j, z)
            remote(
                stage_one.at[k, mine],
                stage_one.at[k, mine],
                sum_send.at[2 * k],
                sum_recv.at[2 * k],
                ctx,
                x,
            ).start()

    def head_sum_next(k):
        settle(stage_one.at[k, pl.ds(0, 7)], sum_recv.at[2 * k])
        total = stage_one[k, 0]
        for j in range(1, 8):
            total = total + stage_one[k, j]
        stage_two[k, x] = total
        for j in range(1, 4):
            remote(
                stage_two.at[k, x],
                stage_two.at[k, x],
                sum_send.at[2 * k + 1],
                sum_recv.at[2 * k + 1],
                place,
                wrapped(x + j, 4),
            ).start()

    def head_sum_end(k):
        settle(stage_two.at[k, pl.ds(0, 3)], sum_recv.at[2 * k + 1])
        return (stage_two[k, 0] + stage_two[k, 1]) + (stage_two[k, 2] + stage_two[k, 3])

    head_sum_start(0, tile_sums(lambda tile: raw[tile] * raw[tile]))

    def turned_part(i, carry):
        rows = part(i)
        scores_turned[rows] = nt(keys[rows], queries[...]).astype(LOW) * inside_turned[rows]
        return carry

    lax.fori_loop(0, parts, turned_part, 0)
    head_sum_next(0)
    settle(landed.at[:, late], data_recv.at[1])
    grads[0:main_slots] = landed[:, late].reshape(main_slots, TILE)
    head_sum_start(1, tile_sums(lambda tile: raw[tile] * grads[tile].astype(F32)))
    total = head_sum_end(0)
    inverse = 1.0 / jnp.sqrt(total / FEATURES + epsilon)
    for t in range(tiles):
        root_wide[t * TILE : (t + 1) * TILE] = turned(inverse[t : t + 1])
    raw[...] = raw[...] * root_wide[...]

    def put(array, i, value):
        sources = PART // main
        if i < main_slots // PART:
            outgoing[i * sources : (i + 1) * sources, array * main : (array + 1) * main] = (
                value.reshape(sources, main, TILE)
            )
        else:
            extra_out[array * 256 : (array + 1) * 256] = value

    for i in range(parts):
        put(0, i, raw[i * PART : (i + 1) * PART].astype(LOW))
    head_sum_next(1)

    def send_back(rows):
        def one(ctx, head, zz):
            remote(
                outgoing.at[ctx, rows], back_ref.at[z, mine, rows], out_send, out_recv, ctx, x
            ).start()

        each_other(one)
        pltpu.make_async_copy(
            outgoing.at[place, rows], back_ref.at[z, mine, rows], out_recv
        ).start()

    send_back(pl.ds(0, main))
    inner = head_sum_end(1) * inverse / FEATURES
    for t in range(tiles):
        inner_wide[t * TILE : (t + 1) * TILE] = turned(inner[t : t + 1])
    dgrads[...] = (
        (grads[...].astype(F32) - raw[...] * inner_wide[...]) * root_wide[...]
    ).astype(LOW)

    back_own[...] = tn(kept_queries[...], dgrads[...])
    for n in (1, 2):
        ctx, unused = at(0, wrapped(z + 8 - n, 8))
        remote(
            back_own, back_all.at[n - 1], state_send.at[1], state_recv.at[n + 1], ctx, x
        ).start()

    for i in range(parts):
        rows = slice(i * PART, (i + 1) * PART)
        mixed = nt(dgrads[rows], values[...]).astype(LOW) * inside[rows]
        kept = dgrads[rows] * carry_low[rows]
        put(1, i, (nn(mixed, keys[...]) + nt(kept, state_low)).astype(LOW))
    send_back(pl.ds(main, main))

    settle(back_all.at[0], state_recv.at[2])
    settle(back_all.at[1], state_recv.at[3])
    back = back_all[0] + goes_on(top + float(GROUP_TOKENS), top) * back_all[1]
    back_low = back.astype(LOW)
    for i in range(parts):
        rows = slice(i * PART, (i + 1) * PART)
        mixed = nt(values[rows], dgrads[...]).astype(LOW) * inside_turned[rows]
        put(2, i, (nn(mixed, queries[...]) + nt(kept_values[rows], back_low)).astype(LOW))
        value_part = nn(scores_turned[rows], dgrads[...]) + nn(kept_keys[rows], back_low)
        put(3, i, value_part.astype(LOW))
    if extra:
        held = extra_out[...]
        blocks = []
        for n in range(4):
            pieces = [held[a * 256 + n * 64 : a * 256 + (n + 1) * 64] for a in range(4)]
            blocks.append(jnp.concatenate(pieces, axis=0))
        extra_rows = nn(spread[...], jnp.concatenate(blocks, axis=1)).astype(LOW)
        for n in range(4):
            outgoing[n * 16 : (n + 1) * 16, 4 * main : rows_all] = extra_rows[
                :, n * TILE : (n + 1) * TILE
            ].reshape(16, 4 * extra, TILE)
    send_back(pl.ds(2 * main, 2 * main + 4 * extra))

    settle(load_all.at[pl.ds(0, 7)], load_sem.at[0])

    @pl.when(owner != z)
    def _():
        settle(load_own, load_sem.at[1])

    settle(packed.at[pl.ds(0, 63)], data_send)
    settle(state_all, state_send.at[0])
    settle(back_all, state_send.at[1])
    for k in range(2):
        settle(stage_one.at[k, pl.ds(0, 7)], sum_send.at[2 * k])
        settle(stage_two.at[k, pl.ds(0, 3)], sum_send.at[2 * k + 1])
    settle(outgoing.at[pl.ds(0, 63)], out_send)
    settle(outgoing, out_recv)


def unpack_kernel(sizes, chain_ref, back_ref, attended_ref, query_ref, key_ref, value_ref):
    main, extra = sizes
    rows_all = 4 * (main + extra)
    group, rank = group_and_rank(chain_ref[...].astype(F32), 1)
    number = iota((TILE, GROUPS * rows_all), 1).astype(F32)
    picks = []
    for a in range(4):
        row = jnp.where(rank < main, a * main + rank, 4 * main + a * extra + rank - main)
        picks.append(ones_where(group * rows_all + row == number).astype(LOW))
    pick = jnp.concatenate(picks, axis=0)
    for head in range(HEADS_HERE):
        found = nn(pick, back_ref[:, head].reshape(GROUPS * rows_all, TILE)).astype(LOW)
        lanes = slice(head * TILE, (head + 1) * TILE)
        for a, ref in enumerate((attended_ref, query_ref, key_ref, value_ref)):
            ref[:, lanes] = found[a * TILE : (a + 1) * TILE]


def layer(sizes, query_in, key_in, value_in, out_grad, chain_order, load_order, doc_lengths):
    main, extra = sizes
    rows_all, slots = 4 * (main + extra), SOURCES * (main + extra)
    chain_row = chain_order.reshape(1, TILE)
    whole = pl.BlockSpec(memory_space=pltpu.VMEM)
    anywhere = pl.BlockSpec(memory_space=pl.ANY)
    wide = pltpu.VMEM((slots, TILE), F32)
    low = pltpu.VMEM((slots, TILE), LOW)
    square = pltpu.VMEM((slots, slots), LOW)
    blocks = pltpu.VMEM((SOURCES, rows_all, TILE), LOW)
    dma = pltpu.SemaphoreType.DMA
    returned = pl.pallas_call(
        functools.partial(fused_kernel, sizes),
        out_shape=jax.ShapeDtypeStruct((GROUPS, HEADS_HERE, rows_all, TILE), LOW),
        in_specs=[anywhere] * 4 + [whole] * 3,
        out_specs=anywhere,
        scratch_shapes=[
            pltpu.VMEM((4 * TILE, HEADS_HERE * TILE), LOW),
            blocks,
            blocks,
            blocks,
            pltpu.VMEM((8, TILE), jnp.int32),
            pltpu.VMEM((8, 8, TILE), jnp.int32),
            pltpu.VMEM((PART, PART), LOW),
            pltpu.VMEM((PART, PART), LOW),
            low,
            low,
            square,
            square,
            wide,
            wide,
            pltpu.VMEM((8, slots), F32),
            low,
            low,
            low,
            low,
            low,
            low,
            low,
            low,
            wide,
            pltpu.VMEM((1024, TILE), LOW),
            square,
            pltpu.VMEM((TILE, TILE), F32),
            pltpu.VMEM((2, TILE, TILE), F32),
            pltpu.VMEM((TILE, TILE), F32),
            pltpu.VMEM((2, TILE, TILE), F32),
            pltpu.VMEM((2, 8, 16, TILE), F32),
            pltpu.VMEM((2, 4, 16, TILE), F32),
            dma((4,)),
            dma((3,)),
            dma,
            dma((2,)),
            dma((2,)),
            dma((4,)),
            dma((4,)),
            dma((4,)),
            dma,
            dma,
        ],
        compiler_params=pltpu.CompilerParams(
            collective_id=1 if extra else 2, has_side_effects=True, vmem_limit_bytes=62 << 20
        ),
        name="fused",
    )(
        query_in,
        key_in,
        value_in,
        out_grad,
        chain_row,
        load_order.reshape(1, TILE),
        doc_lengths.reshape(1, TILE),
    )
    out = jax.ShapeDtypeStruct((TILE, HEADS_HERE * TILE), LOW)
    return pl.pallas_call(
        functools.partial(unpack_kernel, sizes),
        out_shape=(out,) * 4,
        in_specs=[whole] * 2,
        out_specs=(whole,) * 4,
        compiler_params=pltpu.CompilerParams(vmem_limit_bytes=62 << 20),
        name="unpack",
    )(chain_row, returned)


def body(query_in, key_in, value_in, out_grad, chain_order, load_order, doc_lengths):
    ahead = jnp.mod(chain_order // TILE - lax.axis_index("ctx"), SOURCES)
    windows = jnp.mod(ahead[None, :] - jnp.arange(SOURCES)[:, None], SOURCES) < GROUPS
    most = jnp.max(jnp.sum(windows.astype(jnp.int32), axis=1))
    return lax.cond(
        most <= sum(SMALL),
        functools.partial(layer, SMALL),
        functools.partial(layer, LARGE),
        query_in,
        key_in,
        value_in,
        out_grad,
        chain_order,
        load_order,
        doc_lengths,
    )


def solution(mesh):
    return jax.shard_map(
        body,
        mesh=mesh,
        in_specs=(
            P("ctx", "head"),
            P("ctx", "head"),
            P("ctx", "head"),
            P("ctx", "head"),
            P("ctx"),
            P("ctx"),
            P(),
        ),
        out_specs=(P("ctx", "head"), P("ctx", "head"), P("ctx", "head"), P("ctx", "head")),
        check_vma=False,
    )
```

time: 114 us -> 101 us (0.89)
  between operations: 14.7 us -> 1.29 us
where the time goes in v2:
time: 101 us
  Pallas kernels  98 us (97%)
  other arithmetic  1.44 us (1%)
  between operations  1.29 us (1%)
    pallas_call x1, Pallas kernels, layer(): pl.pallas_call(functools.partial(fused_kernel, sizes), out_shape=jax.Shap...  94 us
    pallas_call x1, Pallas kernels, layer(): pl.pallas_call(functools.partial(unpack_kernel, sizes), out_shape=(out,)...  3.98 us

profile of v2, /device:TPU:1, one launch (start us, length us, event | category | flops | bytes accessed | tf_op | source)
XLA Modules:
  0.0 100.9 jit_solution(2557608400879916595)
XLA Ops:
  0.6 0.7 and_select_fusion
  1.3 0.1 convert_reduce_fusion
  1.4 0.6 reduce_max.9
  2.7 98.2 %conditional.1 = ((bf16[128,1024]{1,0:T(8,128)(2,1)}, bf16[128,1024]{1,0:T(8,128)(2,1)}, bf16[128,1024]{1,0:T(8,128)(2,1)}, bf16[128,1024]{1,0:T(8,128)(2,1)})) conditional(s32[]{:T(128)} %convert_element_type.7, (s32[128]{0:T(128)}, s32[128]{0:T(128)}, s32[128]{0:T(128)}, bf16[128,1024]{1,0:T(8,128)(2,1)}, bf16[128,1024]{1,0:T(8,128)(2,1)}, ...), branch_computations={%region_2.3_spmd, %region_3.4_spmd} | conditional | bytes 2084 | solution.py:612
  2.9 0.0 copy-start.1
  2.9 94.0 %fused.3.back_ref = bf16[8,8,80,128]{3,2,1,0:T(8,128)(2,1)} custom-call(bf16[128,1024]{1,0:T(8,128)(2,1)} %get-tuple-element.36.query_hbm, bf16[128,1024]{1,0:T(8,128)(2,1)} %get-tuple-element.37.key_hbm, bf16[128,1024]{1,0:T(8,128)(2,1)} %get-tuple-element.38.value_hbm, bf16[128,1024]{1,0:T(8,128)(2,1)} %get-tuple-element.39.grad_hbm, s32[1,128]{1,0:T(1,128)} %bitcast.8, ...), custom_call_target="tpu_custom_call" | custom-call | tf_op jit(solution)/shard_map/cond/branch_1_fun/fused/pallas_call | solution.py:535
  96.9 0.0 copy-done.1
  97.0 4.0 %unpack.3 = (bf16[128,1024]{1,0:T(8,128)(2,1)}, bf16[128,1024]{1,0:T(8,128)(2,1)}, bf16[128,1024]{1,0:T(8,128)(2,1)}, bf16[128,1024]{1,0:T(8,128)(2,1)}) custom-call(s32[1,128]{1,0:T(1,128)S(1)} %bitcast.9, bf16[8,8,80,128]{3,2,1,0:T(8,128)(2,1)} %fused.3.back_ref), custom_call_target="tpu_custom_call" | custom-call | tf_op jit(solution)/shard_map/cond/branch_1_fun/unpack/pallas_call | solution.py:598
Async XLA Ops:
  2.9 94.1 %copy-start.1 = (s32[128]{0:T(128)S(1)}, s32[128]{0:T(128)}, u32[]{:S(2)}) copy-start(s32[128]{0:T(128)} %get-tuple-element.35) | copy-start | bytes 1540 | tf_op jit(solution)/shard_map/cond

commit v3 on v2

--- a/solution.py
+++ b/solution.py
@@ -76,6 +76,7 @@
     load_ref,
     length_ref,
     back_ref,
+    roots_ref,
     rows_in,
     packed,
     landed,
@@ -108,6 +109,8 @@
     back_all,
     stage_one,
     stage_two,
+    root_tile,
+    root_sem,
     in_sem,
     load_sem,
     data_send,
@@ -141,17 +144,20 @@
     def at(j, zz):
         return plane[j][0] + 2 * zz, plane[j][1]
 
+    def height(i):
+        half = (i + 1) // 2
+        return wrapped(z + jnp.where(lax.rem(i, 2) == 1, 4 - half, 4 + half), 8)
+
     def each_other(act):
-        for j in range(1, 8):
-            act(*at(j, z), z)
-
         def level(i, carry):
-            zz = wrapped(z + i, 8)
+            zz = height(i)
             for j in range(8):
                 act(*at(j, zz), zz)
             return carry
 
-        lax.fori_loop(1, 8, level, 0)
+        lax.fori_loop(0, 7, level, 0)
+        for j in range(1, 8):
+            act(*at(j, z), z)
 
     def remote(src, dst, send, recv, ctx, head):
         return pltpu.make_async_remote_copy(
@@ -226,7 +232,7 @@
         ).start()
 
     def pack_group(i, carry):
-        goal = wrapped(z + i + 1, 8)
+        goal = height(i)
         pick = ones_where(row_number + goal * rows_all == target).astype(LOW)
         block = nn(pick, rows_in[...]).astype(LOW)
         for head in range(HEADS_HERE):
@@ -335,7 +341,7 @@
                 ]
 
     kept_keys[...] = keys[...] * onward_low[...]
-    state_own[...] = tn(kept_keys[...], values[...])
+    state_own[...] = tn(kept_keys[...], values[...]).astype(LOW)
     for n in (1, 2):
         ctx, unused = at(0, wrapped(z + n, 8))
         remote(
@@ -353,9 +359,36 @@
     lax.fori_loop(0, parts, forward_part, 0)
     settle(state_all.at[0], state_recv.at[0])
     settle(state_all.at[1], state_recv.at[1])
-    state = state_all[0] + goes_on(base, base - float(GROUP_TOKENS)) * state_all[1]
+    before = goes_on(base, base - float(GROUP_TOKENS))
+    state = state_all[0].astype(F32) + before * state_all[1].astype(F32)
     state_low = state.astype(LOW)
-    raw[...] = raw[...] + nn(kept_queries[...], state_low)
+
+    def put(array, i, value):
+        sources = PART // main
+        if i < main_slots // PART:
+            outgoing[i * sources : (i + 1) * sources, array * main : (array + 1) * main] = (
+                value.reshape(sources, main, TILE)
+            )
+        else:
+            extra_out[array * 256 : (array + 1) * 256] = value
+
+    def send_back(rows):
+        def one(ctx, head, zz):
+            remote(
+                outgoing.at[ctx, rows], back_ref.at[z, mine, rows], out_send, out_recv, ctx, x
+            ).start()
+
+        each_other(one)
+        pltpu.make_async_copy(
+            outgoing.at[place, rows], back_ref.at[z, mine, rows], out_recv
+        ).start()
+
+    for i in range(parts):
+        rows = slice(i * PART, (i + 1) * PART)
+        whole = raw[rows] + nn(kept_queries[rows], state_low)
+        raw[rows] = whole
+        put(0, i, whole.astype(LOW))
+    send_back(pl.ds(0, main))
 
     def tile_sums(product):
         row = iota((16, TILE), 0)
@@ -368,40 +401,14 @@
             total = jnp.where(row == t, nt(ones, high) + nt(ones, rest), total)
         return total
 
-    def head_sum_start(k, partial):
-        stage_one[k, mine] = partial
-        for j in range(1, 8):
-            ctx, unused = at(j, z)
-            remote(
-                stage_one.at[k, mine],
-                stage_one.at[k, mine],
-                sum_send.at[2 * k],
-                sum_recv.at[2 * k],
-                ctx,
-                x,
-            ).start()
-
-    def head_sum_next(k):
-        settle(stage_one.at[k, pl.ds(0, 7)], sum_recv.at[2 * k])
-        total = stage_one[k, 0]
-        for j in range(1, 8):
-            total = total + stage_one[k, j]
-        stage_two[k, x] = total
-        for j in range(1, 4):
-            remote(
-                stage_two.at[k, x],
-                stage_two.at[k, x],
-                sum_send.at[2 * k + 1],
-                sum_recv.at[2 * k + 1],
-                place,
-                wrapped(x + j, 4),
-            ).start()
-
-    def head_sum_end(k):
-        settle(stage_two.at[k, pl.ds(0, 3)], sum_recv.at[2 * k + 1])
-        return (stage_two[k, 0] + stage_two[k, 1]) + (stage_two[k, 2] + stage_two[k, 3])
-
-    head_sum_start(0, tile_sums(lambda tile: raw[tile] * raw[tile]))
+    settle(landed.at[:, late], data_recv.at[1])
+    grads[0:main_slots] = landed[:, late].reshape(main_slots, TILE)
+    stage_one[mine, 0] = tile_sums(lambda tile: raw[tile] * raw[tile])
+    stage_one[mine, 1] = tile_sums(lambda tile: raw[tile] * grads[tile].astype(F32))
+    for j in range(1, 8):
+        ctx, unused = at(j, z)
+        own = stage_one.at[mine]
+        remote(own, own, sum_send.at[0], sum_recv.at[0], ctx, x).start()
 
     def turned_part(i, carry):
         rows = part(i)
@@ -409,54 +416,49 @@
         return carry
 
     lax.fori_loop(0, parts, turned_part, 0)
-    head_sum_next(0)
-    settle(landed.at[:, late], data_recv.at[1])
-    grads[0:main_slots] = landed[:, late].reshape(main_slots, TILE)
-    head_sum_start(1, tile_sums(lambda tile: raw[tile] * grads[tile].astype(F32)))
-    total = head_sum_end(0)
-    inverse = 1.0 / jnp.sqrt(total / FEATURES + epsilon)
+    settle(stage_one.at[pl.ds(0, 7)], sum_recv.at[0])
+    partial = stage_one[0]
+    for j in range(1, 8):
+        partial = partial + stage_one[j]
+    stage_two[x] = partial
+    for j in range(1, 4):
+        own = stage_two.at[x]
+        remote(own, own, sum_send.at[1], sum_recv.at[1], place, wrapped(x + j, 4)).start()
+    settle(stage_two.at[pl.ds(0, 3)], sum_recv.at[1])
+    total = (stage_two[0] + stage_two[1]) + (stage_two[2] + stage_two[3])
+    inverse = 1.0 / jnp.sqrt(total[0] / FEATURES + epsilon)
+    inner = total[1] * inverse / FEATURES
+    root_tile[...] = inverse
+    scale = inverse * inner
     for t in range(tiles):
         root_wide[t * TILE : (t + 1) * TILE] = turned(inverse[t : t + 1])
-    raw[...] = raw[...] * root_wide[...]
-
-    def put(array, i, value):
-        sources = PART // main
-        if i < main_slots // PART:
-            outgoing[i * sources : (i + 1) * sources, array * main : (array + 1) * main] = (
-                value.reshape(sources, main, TILE)
-            )
-        else:
-            extra_out[array * 256 : (array + 1) * 256] = value
-
-    for i in range(parts):
-        put(0, i, raw[i * PART : (i + 1) * PART].astype(LOW))
-    head_sum_next(1)
-
-    def send_back(rows):
-        def one(ctx, head, zz):
-            remote(
-                outgoing.at[ctx, rows], back_ref.at[z, mine, rows], out_send, out_recv, ctx, x
-            ).start()
-
-        each_other(one)
-        pltpu.make_async_copy(
-            outgoing.at[place, rows], back_ref.at[z, mine, rows], out_recv
-        ).start()
-
-    send_back(pl.ds(0, main))
-    inner = head_sum_end(1) * inverse / FEATURES
-    for t in range(tiles):
-        inner_wide[t * TILE : (t + 1) * TILE] = turned(inner[t : t + 1])
+        inner_wide[t * TILE : (t + 1) * TILE] = turned(scale[t : t + 1])
     dgrads[...] = (
         (grads[...].astype(F32) - raw[...] * inner_wide[...]) * root_wide[...]
     ).astype(LOW)
 
-    back_own[...] = tn(kept_queries[...], dgrads[...])
+    back_own[...] = tn(kept_queries[...], dgrads[...]).astype(LOW)
     for n in (1, 2):
         ctx, unused = at(0, wrapped(z + 8 - n, 8))
         remote(
             back_own, back_all.at[n - 1], state_send.at[1], state_recv.at[n + 1], ctx, x
         ).start()
+
+    for j in range(8):
+        ctx = wrapped(place // 8 + j, 8) * 8 + mine
+        if j == 0:
+
+            @pl.when(ctx == place)
+            def _():
+                pltpu.make_async_copy(root_tile, roots_ref.at[z], root_sem.at[2]).start()
+
+            @pl.when(ctx != place)
+            def _():
+                remote(
+                    root_tile, roots_ref.at[z], root_sem.at[1], root_sem.at[2], ctx, x
+                ).start()
+        else:
+            remote(root_tile, roots_ref.at[z], root_sem.at[0], root_sem.at[2], ctx, x).start()
 
     for i in range(parts):
         rows = slice(i * PART, (i + 1) * PART)
@@ -467,7 +469,8 @@
 
     settle(back_all.at[0], state_recv.at[2])
     settle(back_all.at[1], state_recv.at[3])
-    back = back_all[0] + goes_on(top + float(GROUP_TOKENS), top) * back_all[1]
+    after = goes_on(top + float(GROUP_TOKENS), top)
+    back = back_all[0].astype(F32) + after * back_all[1].astype(F32)
     back_low = back.astype(LOW)
     for i in range(parts):
         rows = slice(i * PART, (i + 1) * PART)
@@ -497,28 +500,53 @@
     settle(packed.at[pl.ds(0, 63)], data_send)
     settle(state_all, state_send.at[0])
     settle(back_all, state_send.at[1])
-    for k in range(2):
-        settle(stage_one.at[k, pl.ds(0, 7)], sum_send.at[2 * k])
-        settle(stage_two.at[k, pl.ds(0, 3)], sum_send.at[2 * k + 1])
+    settle(stage_one.at[pl.ds(0, 7)], sum_send.at[0])
+    settle(stage_two.at[pl.ds(0, 3)], sum_send.at[1])
+    settle(roots_ref.at[pl.ds(0, 7)], root_sem.at[0])
+
+    @pl.when(wrapped(place // 8, 8) * 8 + mine != place)
+    def _():
+        settle(root_tile, root_sem.at[1])
+
+    settle(roots_ref, root_sem.at[2])
     settle(outgoing.at[pl.ds(0, 63)], out_send)
     settle(outgoing, out_recv)
 
 
-def unpack_kernel(sizes, chain_ref, back_ref, attended_ref, query_ref, key_ref, value_ref):
+def unpack_kernel(
+    sizes, chain_ref, back_ref, roots_ref, attended_ref, query_ref, key_ref, value_ref, pick, factor
+):
     main, extra = sizes
     rows_all = 4 * (main + extra)
-    group, rank = group_and_rank(chain_ref[...].astype(F32), 1)
-    number = iota((TILE, GROUPS * rows_all), 1).astype(F32)
-    picks = []
-    for a in range(4):
-        row = jnp.where(rank < main, a * main + rank, 4 * main + a * extra + rank - main)
-        picks.append(ones_where(group * rows_all + row == number).astype(LOW))
-    pick = jnp.concatenate(picks, axis=0)
-    for head in range(HEADS_HERE):
-        found = nn(pick, back_ref[:, head].reshape(GROUPS * rows_all, TILE)).astype(LOW)
+
+    @pl.when(pl.program_id(0) == 0)
+    def _():
+        place = lax.axis_index("ctx")
+        group, rank = group_and_rank(chain_ref[...].astype(F32), 1)
+        number = iota((TILE, GROUPS * rows_all), 1).astype(F32)
+        for a in range(4):
+            row = jnp.where(rank < main, a * main + rank, 4 * main + a * extra + rank - main)
+            pick[a * TILE : (a + 1) * TILE] = ones_where(
+                group * rows_all + row == number
+            ).astype(LOW)
+        lane = iota((TILE, TILE), 1).astype(F32)
+        kinds = [(place * main, rank, rank < main)]
+        if extra:
+            kinds.append((SOURCES * main + place * extra, rank - main, rank >= main))
+        found = jnp.zeros((TILE, TILE), F32)
+        for first, at_slot, chosen in kinds:
+            wanted = jnp.where(chosen, lax.rem(first, TILE).astype(F32) + at_slot, -1.0)
+            for g in range(GROUPS):
+                row = roots_ref[g, pl.ds(first // TILE, 1)]
+                found = found + jnp.where((group == g) & (wanted == lane), row, 0.0)
+        factor[...] = jnp.broadcast_to(jnp.sum(found, axis=1, keepdims=True), (TILE, TILE))
+
+    for head in range(2):
+        found = nn(pick[...], back_ref[:, head].reshape(GROUPS * rows_all, TILE))
         lanes = slice(head * TILE, (head + 1) * TILE)
-        for a, ref in enumerate((attended_ref, query_ref, key_ref, value_ref)):
-            ref[:, lanes] = found[a * TILE : (a + 1) * TILE]
+        attended_ref[:, lanes] = (found[0:TILE] * factor[...]).astype(LOW)
+        for a, ref in enumerate((query_ref, key_ref, value_ref)):
+            ref[:, lanes] = found[(a + 1) * TILE : (a + 2) * TILE].astype(LOW)
 
 
 def layer(sizes, query_in, key_in, value_in, out_grad, chain_order, load_order, doc_lengths):
@@ -532,11 +560,14 @@
     square = pltpu.VMEM((slots, slots), LOW)
     blocks = pltpu.VMEM((SOURCES, rows_all, TILE), LOW)
     dma = pltpu.SemaphoreType.DMA
-    returned = pl.pallas_call(
+    returned, roots = pl.pallas_call(
         functools.partial(fused_kernel, sizes),
-        out_shape=jax.ShapeDtypeStruct((GROUPS, HEADS_HERE, rows_all, TILE), LOW),
+        out_shape=(
+            jax.ShapeDtypeStruct((GROUPS, HEADS_HERE, rows_all, TILE), LOW),
+            jax.ShapeDtypeStruct((GROUPS, 16, TILE), F32),
+        ),
         in_specs=[anywhere] * 4 + [whole] * 3,
-        out_specs=anywhere,
+        out_specs=(anywhere, anywhere),
         scratch_shapes=[
             pltpu.VMEM((4 * TILE, HEADS_HERE * TILE), LOW),
             blocks,
@@ -564,20 +595,22 @@
             wide,
             pltpu.VMEM((1024, TILE), LOW),
             square,
-            pltpu.VMEM((TILE, TILE), F32),
-            pltpu.VMEM((2, TILE, TILE), F32),
-            pltpu.VMEM((TILE, TILE), F32),
-            pltpu.VMEM((2, TILE, TILE), F32),
-            pltpu.VMEM((2, 8, 16, TILE), F32),
-            pltpu.VMEM((2, 4, 16, TILE), F32),
+            pltpu.VMEM((TILE, TILE), LOW),
+            pltpu.VMEM((2, TILE, TILE), LOW),
+            pltpu.VMEM((TILE, TILE), LOW),
+            pltpu.VMEM((2, TILE, TILE), LOW),
+            pltpu.VMEM((8, 2, 16, TILE), F32),
+            pltpu.VMEM((4, 2, 16, TILE), F32),
+            pltpu.VMEM((16, TILE), F32),
+            dma((3,)),
             dma((4,)),
             dma((3,)),
             dma,
             dma((2,)),
             dma((2,)),
             dma((4,)),
-            dma((4,)),
-            dma((4,)),
+            dma((2,)),
+            dma((2,)),
             dma,
             dma,
         ],
@@ -595,14 +628,24 @@
         doc_lengths.reshape(1, TILE),
     )
     out = jax.ShapeDtypeStruct((TILE, HEADS_HERE * TILE), LOW)
+    out_block = pl.BlockSpec((TILE, 2 * TILE), lambda i: (0, i))
     return pl.pallas_call(
         functools.partial(unpack_kernel, sizes),
+        grid=(HEADS_HERE // 2,),
         out_shape=(out,) * 4,
-        in_specs=[whole] * 2,
-        out_specs=(whole,) * 4,
+        in_specs=[
+            pl.BlockSpec((1, TILE), lambda i: (0, 0)),
+            pl.BlockSpec((GROUPS, 2, rows_all, TILE), lambda i: (0, i, 0, 0)),
+            pl.BlockSpec((GROUPS, 16, TILE), lambda i: (0, 0, 0)),
+        ],
+        out_specs=(out_block,) * 4,
+        scratch_shapes=[
+            pltpu.VMEM((4 * TILE, GROUPS * rows_all), LOW),
+            pltpu.VMEM((TILE, TILE), F32),
+        ],
         compiler_params=pltpu.CompilerParams(vmem_limit_bytes=62 << 20),
         name="unpack",
-    )(chain_row, returned)
+    )(chain_row, returned, roots)
 
 
 def body(query_in, key_in, value_in, out_grad, chain_order, load_order, doc_lengths):

time: 101 us -> 94.8 us (0.939)
  Pallas kernels: 98 us -> 91.6 us
    pallas_call x2, Pallas kernels: 98 us -> 91.6 us  [the longest x1 86.6 us: layer(): pl.pallas_call(functools.partial(fused_kernel, sizes), out_shape=(jax.Sha...]
where the time goes in v3:
time: 94.8 us; the launch traced here: 94.6 us
  Pallas kernels  91.6 us (97%)
  other arithmetic  1.44 us (2%)
  between operations  1.42 us (1%)
    pallas_call x1, Pallas kernels, layer(): pl.pallas_call(functools.partial(fused_kernel, sizes), out_shape=(jax.Sha...  86.6 us
    pallas_call x1, Pallas kernels, layer(): pl.pallas_call(functools.partial(unpack_kernel, sizes), grid=(HEADS_HERE...  4.99 us

profile of v3, /device:TPU:1, one launch (start us, length us, event | category | flops | bytes accessed | tf_op | source)
XLA Modules:
  0.0 94.6 jit_solution(8245798931993637091)
XLA Ops:
  0.6 0.7 and_select_fusion
  1.3 0.1 convert_reduce_fusion
  1.4 0.6 reduce_max.9
  2.7 91.7 %conditional.1 = ((bf16[128,1024]{1,0:T(8,128)(2,1)}, bf16[128,1024]{1,0:T(8,128)(2,1)}, bf16[128,1024]{1,0:T(8,128)(2,1)}, bf16[128,1024]{1,0:T(8,128)(2,1)})) conditional(s32[]{:T(128)} %convert_element_type.7, (s32[128]{0:T(128)}, s32[128]{0:T(128)}, s32[128]{0:T(128)}, bf16[128,1024]{1,0:T(8,128)(2,1)}, bf16[128,1024]{1,0:T(8,128)(2,1)}, ...), branch_computations={%region_2.3_spmd, %region_3.4_spmd} | conditional | bytes 8 | solution.py:655
  2.9 86.6 %fused.3 = (bf16[8,8,80,128]{3,2,1,0:T(8,128)(2,1)}, f32[8,16,128]{2,1,0:T(8,128)}) custom-call(bf16[128,1024]{1,0:T(8,128)(2,1)} %get-tuple-element.38.query_hbm, bf16[128,1024]{1,0:T(8,128)(2,1)} %get-tuple-element.39.key_hbm, bf16[128,1024]{1,0:T(8,128)(2,1)} %get-tuple-element.40.value_hbm, bf16[128,1024]{1,0:T(8,128)(2,1)} %get-tuple-element.41.grad_hbm, ...), custom_call_target="tpu_custom_call" | custom-call | tf_op jit(solution)/shard_map/cond/branch_1_fun/fused/pallas_call | solution.py:563
  89.5 5.0 %unpack.3 = (bf16[128,1024]{1,0:T(8,128)(2,1)}, bf16[128,1024]{1,0:T(8,128)(2,1)}, bf16[128,1024]{1,0:T(8,128)(2,1)}, bf16[128,1024]{1,0:T(8,128)(2,1)}) custom-call(s32[1,128]{1,0:T(1,128)} %bitcast.9, bf16[8,8,80,128]{3,2,1,0:T(8,128)(2,1)} %get-tuple-element.44.back_ref, f32[8,16,128]{2,1,0:T(8,128)} %get-tuple-element.45.roots_ref), custom_call_target="tpu_custom_call" | custom-call | tf_op jit(solution)/shard_map/cond/branch_1_fun/unpack/pallas_call | solution.py:632

commit v4 on v3

--- a/solution.py
+++ b/solution.py
@@ -388,7 +388,6 @@
         whole = raw[rows] + nn(kept_queries[rows], state_low)
         raw[rows] = whole
         put(0, i, whole.astype(LOW))
-    send_back(pl.ds(0, main))
 
     def tile_sums(product):
         row = iota((16, TILE), 0)
@@ -409,6 +408,8 @@
         ctx, unused = at(j, z)
         own = stage_one.at[mine]
         remote(own, own, sum_send.at[0], sum_recv.at[0], ctx, x).start()
+
+    send_back(pl.ds(0, main))
 
     def turned_part(i, carry):
         rows = part(i)
@@ -514,39 +515,64 @@
 
 
 def unpack_kernel(
-    sizes, chain_ref, back_ref, roots_ref, attended_ref, query_ref, key_ref, value_ref, pick, factor
+    sizes,
+    chain_hbm,
+    back_hbm,
+    roots_hbm,
+    attended_hbm,
+    query_hbm,
+    key_hbm,
+    value_hbm,
+    chain_ref,
+    roots_ref,
+    back,
+    out,
+    pick,
+    in_sem,
+    out_sem,
 ):
     main, extra = sizes
     rows_all = 4 * (main + extra)
-
-    @pl.when(pl.program_id(0) == 0)
-    def _():
-        place = lax.axis_index("ctx")
-        group, rank = group_and_rank(chain_ref[...].astype(F32), 1)
-        number = iota((TILE, GROUPS * rows_all), 1).astype(F32)
-        for a in range(4):
-            row = jnp.where(rank < main, a * main + rank, 4 * main + a * extra + rank - main)
-            pick[a * TILE : (a + 1) * TILE] = ones_where(
-                group * rows_all + row == number
-            ).astype(LOW)
-        lane = iota((TILE, TILE), 1).astype(F32)
-        kinds = [(place * main, rank, rank < main)]
-        if extra:
-            kinds.append((SOURCES * main + place * extra, rank - main, rank >= main))
-        found = jnp.zeros((TILE, TILE), F32)
-        for first, at_slot, chosen in kinds:
-            wanted = jnp.where(chosen, lax.rem(first, TILE).astype(F32) + at_slot, -1.0)
-            for g in range(GROUPS):
-                row = roots_ref[g, pl.ds(first // TILE, 1)]
-                found = found + jnp.where((group == g) & (wanted == lane), row, 0.0)
-        factor[...] = jnp.broadcast_to(jnp.sum(found, axis=1, keepdims=True), (TILE, TILE))
-
-    for head in range(2):
-        found = nn(pick[...], back_ref[:, head].reshape(GROUPS * rows_all, TILE))
-        lanes = slice(head * TILE, (head + 1) * TILE)
-        attended_ref[:, lanes] = (found[0:TILE] * factor[...]).astype(LOW)
-        for a, ref in enumerate((query_ref, key_ref, value_ref)):
-            ref[:, lanes] = found[(a + 1) * TILE : (a + 2) * TILE].astype(LOW)
+    outputs = (attended_hbm, query_hbm, key_hbm, value_hbm)
+    pairs = [pl.ds(2 * n, 2) for n in range(HEADS_HERE // 2)]
+    pltpu.make_async_copy(chain_hbm, chain_ref, in_sem.at[4]).start()
+    pltpu.make_async_copy(roots_hbm, roots_ref, in_sem.at[5]).start()
+    for n, pair in enumerate(pairs):
+        pltpu.make_async_copy(back_hbm.at[:, pair], back.at[:, pair], in_sem.at[n]).start()
+    place = lax.axis_index("ctx")
+    pltpu.make_async_copy(chain_hbm, chain_ref, in_sem.at[4]).wait()
+    group, rank = group_and_rank(chain_ref[...].astype(F32), 1)
+    number = iota((TILE, GROUPS * rows_all), 1).astype(F32)
+    for a in range(4):
+        row = jnp.where(rank < main, a * main + rank, 4 * main + a * extra + rank - main)
+        pick[a * TILE : (a + 1) * TILE] = ones_where(group * rows_all + row == number).astype(LOW)
+    lane = iota((TILE, TILE), 1).astype(F32)
+    kinds = [(place * main, rank, rank < main)]
+    if extra:
+        kinds.append((SOURCES * main + place * extra, rank - main, rank >= main))
+    spot = jnp.zeros((TILE, TILE), F32)
+    pltpu.make_async_copy(roots_hbm, roots_ref, in_sem.at[5]).wait()
+    for first, at_slot, chosen in kinds:
+        wanted = jnp.where(chosen, lax.rem(first, TILE).astype(F32) + at_slot, -1.0)
+        rows = jnp.zeros((TILE, TILE), F32)
+        for g in range(GROUPS):
+            rows = jnp.where(group == g, roots_ref[g, pl.ds(first // TILE, 1)], rows)
+        spot = spot + jnp.where(wanted == lane, rows, 0.0)
+    factor = jnp.sum(spot, axis=1, keepdims=True)
+
+    for n, pair in enumerate(pairs):
+        pltpu.make_async_copy(back_hbm.at[:, pair], back.at[:, pair], in_sem.at[n]).wait()
+        both = [back[:, 2 * n + k].reshape(GROUPS * rows_all, TILE) for k in range(2)]
+        found = nn(pick[...], jnp.concatenate(both, axis=1))
+        lanes = pl.ds(2 * n * TILE, 2 * TILE)
+        for a, ref in enumerate(outputs):
+            block = found[a * TILE : (a + 1) * TILE]
+            out[a, :, lanes] = (block * factor if a == 0 else block).astype(LOW)
+            pltpu.make_async_copy(out.at[a, :, lanes], ref.at[:, lanes], out_sem.at[a, n]).start()
+    for n in range(HEADS_HERE // 2):
+        lanes = pl.ds(2 * n * TILE, 2 * TILE)
+        for a, ref in enumerate(outputs):
+            pltpu.make_async_copy(out.at[a, :, lanes], ref.at[:, lanes], out_sem.at[a, n]).wait()
 
 
 def layer(sizes, query_in, key_in, value_in, out_grad, chain_order, load_order, doc_lengths):
@@ -628,32 +654,44 @@
         doc_lengths.reshape(1, TILE),
     )
     out = jax.ShapeDtypeStruct((TILE, HEADS_HERE * TILE), LOW)
-    out_block = pl.BlockSpec((TILE, 2 * TILE), lambda i: (0, i))
     return pl.pallas_call(
         functools.partial(unpack_kernel, sizes),
-        grid=(HEADS_HERE // 2,),
         out_shape=(out,) * 4,
-        in_specs=[
-            pl.BlockSpec((1, TILE), lambda i: (0, 0)),
-            pl.BlockSpec((GROUPS, 2, rows_all, TILE), lambda i: (0, i, 0, 0)),
-            pl.BlockSpec((GROUPS, 16, TILE), lambda i: (0, 0, 0)),
-        ],
-        out_specs=(out_block,) * 4,
+        in_specs=[anywhere] * 3,
+        out_specs=(anywhere,) * 4,
         scratch_shapes=[
+            pltpu.VMEM((1, TILE), jnp.int32),
+            pltpu.VMEM((GROUPS, 16, TILE), F32),
+            pltpu.VMEM((GROUPS, HEADS_HERE, rows_all, TILE), LOW),
+            pltpu.VMEM((4, TILE, HEADS_HERE * TILE), LOW),
             pltpu.VMEM((4 * TILE, GROUPS * rows_all), LOW),
-            pltpu.VMEM((TILE, TILE), F32),
+            dma((6,)),
+            dma((4, 4)),
         ],
         compiler_params=pltpu.CompilerParams(vmem_limit_bytes=62 << 20),
         name="unpack",
     )(chain_row, returned, roots)
 
 
+def most_kernel(chain_ref, most_ref):
+    ahead = chain_ref[...] // TILE - lax.axis_index("ctx")
+    ahead = jnp.where(ahead < 0, ahead + SOURCES, ahead)
+    past = jnp.broadcast_to(ahead, (SOURCES, TILE)) - iota((SOURCES, TILE), 0)
+    past = jnp.where(past < 0, past + SOURCES, past)
+    counts = jnp.sum(ones_where(past < GROUPS), axis=1, keepdims=True)
+    most_ref[0] = jnp.max(counts).astype(jnp.int32)
+
+
 def body(query_in, key_in, value_in, out_grad, chain_order, load_order, doc_lengths):
-    ahead = jnp.mod(chain_order // TILE - lax.axis_index("ctx"), SOURCES)
-    windows = jnp.mod(ahead[None, :] - jnp.arange(SOURCES)[:, None], SOURCES) < GROUPS
-    most = jnp.max(jnp.sum(windows.astype(jnp.int32), axis=1))
+    most = pl.pallas_call(
+        most_kernel,
+        out_shape=jax.ShapeDtypeStruct((1,), jnp.int32),
+        in_specs=[pl.BlockSpec(memory_space=pltpu.VMEM)],
+        out_specs=pl.BlockSpec(memory_space=pltpu.SMEM),
+        name="most",
+    )(chain_order.reshape(1, TILE))
     return lax.cond(
-        most <= sum(SMALL),
+        most[0] <= sum(SMALL),
         functools.partial(layer, SMALL),
         functools.partial(layer, LARGE),
         query_in,

time: 94.8 us -> 92.9 us (0.980)
  other arithmetic: 1.44 us -> 0 us
    pallas_call x1, Pallas kernels: 86.6 us -> 85.4 us  [layer(): pl.pallas_call(functools.partial(fused_kernel, sizes), out_shape=(jax.Sha...]
    pallas_call x1 -> x2, Pallas kernels: 4.99 us -> 5.64 us  [the longest x1 4.33 us: layer(): pl.pallas_call(functools.partial(unpack_kernel, sizes), out_shape=(out,)...]
where the time goes in v4:
time: 92.9 us; the launch traced here: 92.7 us
  Pallas kernels  91.1 us (98%)
  between operations  1.47 us (2%)
    pallas_call x1, Pallas kernels, layer(): pl.pallas_call(functools.partial(fused_kernel, sizes), out_shape=(jax.Sha...  85.4 us
    pallas_call x1, Pallas kernels, layer(): pl.pallas_call(functools.partial(unpack_kernel, sizes), out_shape=(out,)...  4.33 us

profile of v4, /device:TPU:1, one launch (start us, length us, event | category | flops | bytes accessed | tf_op | source)
XLA Modules:
  0.0 92.7 jit_solution(10037159279971870998)
XLA Ops:
  0.6 1.3 %most.1 = s32[1]{0:T(128)} custom-call(s32[1,128]{1,0:T(1,128)} %bitcast.8), custom_call_target="tpu_custom_call" | custom-call | tf_op jit(solution)/shard_map/most/pallas_call | solution.py:686
  2.6 89.9 %conditional.1 = ((bf16[128,1024]{1,0:T(8,128)(2,1)}, bf16[128,1024]{1,0:T(8,128)(2,1)}, bf16[128,1024]{1,0:T(8,128)(2,1)}, bf16[128,1024]{1,0:T(8,128)(2,1)})) conditional(s32[]{:T(128)} %bitcast.7, (s32[128]{0:T(128)}, s32[128]{0:T(128)}, s32[128]{0:T(128)}, bf16[128,1024]{1,0:T(8,128)(2,1)}, bf16[128,1024]{1,0:T(8,128)(2,1)}, ...), branch_computations={%region_0.0_spmd, %region_1.0_spmd} | conditional | bytes 8 | solution.py:693
  2.8 85.4 %fused.3 = (bf16[8,8,80,128]{3,2,1,0:T(8,128)(2,1)}, f32[8,16,128]{2,1,0:T(8,128)}) custom-call(bf16[128,1024]{1,0:T(8,128)(2,1)} %get-tuple-element.38.query_hbm, bf16[128,1024]{1,0:T(8,128)(2,1)} %get-tuple-element.39.key_hbm, bf16[128,1024]{1,0:T(8,128)(2,1)} %get-tuple-element.40.value_hbm, bf16[128,1024]{1,0:T(8,128)(2,1)} %get-tuple-element.41.grad_hbm, ...), custom_call_target="tpu_custom_call" | custom-call | tf_op jit(solution)/shard_map/cond/branch_1_fun/fused/pallas_call | solution.py:589
  88.2 4.3 %unpack.3 = (bf16[128,1024]{1,0:T(8,128)(2,1)}, bf16[128,1024]{1,0:T(8,128)(2,1)}, bf16[128,1024]{1,0:T(8,128)(2,1)}, bf16[128,1024]{1,0:T(8,128)(2,1)}) custom-call(s32[1,128]{1,0:T(1,128)} %bitcast.12, bf16[8,8,80,128]{3,2,1,0:T(8,128)(2,1)} %get-tuple-element.44.back_hbm, f32[8,16,128]{2,1,0:T(8,128)} %get-tuple-element.45.roots_hbm), custom_call_target="tpu_custom_call" | custom-call | tf_op jit(solution)/shard_map/cond/branch_1_fun/unpack/pallas_call | solution.py:657

commit v5 on v4

--- a/solution.py
+++ b/solution.py
@@ -477,6 +477,9 @@
         rows = slice(i * PART, (i + 1) * PART)
         mixed = nt(values[rows], dgrads[...]).astype(LOW) * inside_turned[rows]
         put(2, i, (nn(mixed, queries[...]) + nt(kept_values[rows], back_low)).astype(LOW))
+    send_back(pl.ds(2 * main, main))
+    for i in range(parts):
+        rows = slice(i * PART, (i + 1) * PART)
         value_part = nn(scores_turned[rows], dgrads[...]) + nn(kept_keys[rows], back_low)
         put(3, i, value_part.astype(LOW))
     if extra:
@@ -490,7 +493,7 @@
             outgoing[n * 16 : (n + 1) * 16, 4 * main : rows_all] = extra_rows[
                 :, n * TILE : (n + 1) * TILE
             ].reshape(16, 4 * extra, TILE)
-    send_back(pl.ds(2 * main, 2 * main + 4 * extra))
+    send_back(pl.ds(3 * main, main + 4 * extra))
 
     settle(load_all.at[pl.ds(0, 7)], load_sem.at[0])
 

time: 92.9 us -> 93.6 us (level)
  no operation moved by 1% of the time
where the time goes in v5:
time: 93.6 us; the launch traced here: 93.4 us
  Pallas kernels  91.5 us (98%)
  between operations  1.55 us (2%)
    pallas_call x1, Pallas kernels, layer(): pl.pallas_call(functools.partial(fused_kernel, sizes), out_shape=(jax.Sha...  85.8 us
    pallas_call x1, Pallas kernels, layer(): pl.pallas_call(functools.partial(unpack_kernel, sizes), out_shape=(out,)...  4.33 us

profile of v5, /device:TPU:1, one launch (start us, length us, event | category | flops | bytes accessed | tf_op | source)
XLA Modules:
  0.0 93.4 jit_solution(6672196987277329445)
XLA Ops:
  0.6 1.3 %most.1 = s32[1]{0:T(128)} custom-call(s32[1,128]{1,0:T(1,128)} %bitcast.8), custom_call_target="tpu_custom_call" | custom-call | tf_op jit(solution)/shard_map/most/pallas_call | solution.py:689
  2.6 90.6 %conditional.1 = ((bf16[128,1024]{1,0:T(8,128)(2,1)}, bf16[128,1024]{1,0:T(8,128)(2,1)}, bf16[128,1024]{1,0:T(8,128)(2,1)}, bf16[128,1024]{1,0:T(8,128)(2,1)})) conditional(s32[]{:T(128)} %bitcast.7, (s32[128]{0:T(128)}, s32[128]{0:T(128)}, s32[128]{0:T(128)}, bf16[128,1024]{1,0:T(8,128)(2,1)}, bf16[128,1024]{1,0:T(8,128)(2,1)}, ...), branch_computations={%region_0.0_spmd, %region_1.0_spmd} | conditional | bytes 8 | solution.py:696
  2.8 85.8 %fused.3 = (bf16[8,8,80,128]{3,2,1,0:T(8,128)(2,1)}, f32[8,16,128]{2,1,0:T(8,128)}) custom-call(bf16[128,1024]{1,0:T(8,128)(2,1)} %get-tuple-element.38.query_hbm, bf16[128,1024]{1,0:T(8,128)(2,1)} %get-tuple-element.39.key_hbm, bf16[128,1024]{1,0:T(8,128)(2,1)} %get-tuple-element.40.value_hbm, bf16[128,1024]{1,0:T(8,128)(2,1)} %get-tuple-element.41.grad_hbm, ...), custom_call_target="tpu_custom_call" | custom-call | tf_op jit(solution)/shard_map/cond/branch_1_fun/fused/pallas_call | solution.py:592
  88.6 4.3 %unpack.3 = (bf16[128,1024]{1,0:T(8,128)(2,1)}, bf16[128,1024]{1,0:T(8,128)(2,1)}, bf16[128,1024]{1,0:T(8,128)(2,1)}, bf16[128,1024]{1,0:T(8,128)(2,1)}) custom-call(s32[1,128]{1,0:T(1,128)} %bitcast.12, bf16[8,8,80,128]{3,2,1,0:T(8,128)(2,1)} %get-tuple-element.44.back_hbm, f32[8,16,128]{2,1,0:T(8,128)} %get-tuple-element.45.roots_hbm), custom_call_target="tpu_custom_call" | custom-call | tf_op jit(solution)/shard_map/cond/branch_1_fun/unpack/pallas_call | solution.py:660
